TPU v7x, 256 devices: a whole 4x4x8 slice. The times are simulated.
256 devices in a mesh: outer: 16 (over z_hi, x, core), tp: 16 (over z_lo, y).
Axes of the slice: x: 4, y: 4, z: 8 (z_hi: 2, z_lo: 4; z = z_hi * 4 + z_lo), core: 2. Of those that a mesh axis runs over, the one named last changes fastest.
Arguments:
- delta: bfloat16 [16, 4096, 4096], P('outer', None, 'tp'), may hold values from -6 to 6
- error: bfloat16 [16, 4096, 4096], P('outer', None, 'tp'), may hold values from -6 to 6
- momentum: bfloat16 [4096, 4096], P(None, 'tp'), may hold values from -3 to 3
- q_init: bfloat16 [4096, 256], P('tp'), may hold values from -6 to 6
Outputs:
- new_error: bfloat16 [16, 4096, 4096], P('outer', None, 'tp')
- new_momentum: bfloat16 [4096, 4096], P(None, 'tp')
- outer_step: bfloat16 [4096, 4096], P(None, 'tp')
- new_factor: bfloat16 [4096, 256], P('tp')
All inputs are finite; a program needn't handle non-finite values.
Results may differ from a plain program's by a relative error of at most 0.02.
Values may be sent and summed in bfloat16 or wider, within the bound.
A program may use at most 64 MiB of HBM per device.

v0:
```python
import jax
import jax.numpy as jnp
from jax import lax
from jax.sharding import PartitionSpec as P


def orthonormal(left, lower):
    return lax.linalg.triangular_solve(
        lower, left, left_side=False, lower=True, transpose_a=True
    ).astype(jnp.bfloat16)


def factor_whole(left):
    gram = jnp.dot(left.T, left, precision=lax.Precision.HIGHEST)
    return orthonormal(left, jnp.linalg.cholesky(gram))


def body(delta, error, momentum, q_init):
    merged = (delta[0].astype(jnp.float32) + error[0].astype(jnp.float32)).astype(jnp.bfloat16)
    term = jnp.dot(merged, q_init, preferred_element_type=jnp.float32)
    left = lax.psum(term, ("outer", "tp"))
    basis = factor_whole(left)
    local_right = lax.dot_general(
        merged, basis, (((0,), (0,)), ((), ())), preferred_element_type=jnp.float32
    )
    right = lax.psum(local_right.astype(jnp.bfloat16), "outer").astype(jnp.float32)
    new_factor = (right / lax.axis_size("outer")).astype(jnp.bfloat16)
    approx = jnp.dot(basis, new_factor.T, preferred_element_type=jnp.float32)
    new_error = (merged.astype(jnp.float32) - approx).astype(jnp.bfloat16)[None]
    moment = 0.9 * momentum.astype(jnp.float32) + approx
    outer_step = (0.7 * (approx + 0.9 * moment)).astype(jnp.bfloat16)
    return (new_error, moment.astype(jnp.bfloat16), outer_step, new_factor)


def solution(mesh):
    placed = (P("outer", None, "tp"), P("outer", None, "tp"), P(None, "tp"), P("tp", None))
    return jax.shard_map(
        body,
        mesh=mesh,
        in_specs=placed,
        out_specs=(P("outer", None, "tp"), P(None, "tp"), P(None, "tp"), P("tp", None)),
        check_vma=False,
    )
```

profile of v0, /device:TPU:1, one launch (start us, length us, event | category | flops | bytes accessed | tf_op | source)
XLA Modules:
  0.0 555.9 jit_solution(4328131485737931294)
XLA Ops:
  7.2 0.8 copy-done
  8.1 4.9 fusion.16
  13.1 271.1 %all-reduce.4.cloned.1.call-done = f32[4096,256]{1,0:T(8,128)} async-done(((f32[4096,256]{1,0:T(8,128)}), f32[4096,256]{1,0:T(8,128)}) %all-reduce.4.cloned.1.call-update) | async-done | bytes 4194320 | tf_op jit(solution)/shard_map/psum | solution.py:21
  284.2 10.1 %fusion.20 = f32[256,256]{1,0:T(8,128)S(1)} fusion(f32[4096,256]{1,0:T(8,128)} %all-reduce.4.cloned.1.call-done), kind=kOutput, calls=%fused_computation.44 | convolution fusion | flops 3221225472 | bytes 4456448 | tf_op jit(solution)/shard_map/dot_general | solution.py:14
  294.3 0.1 copy.8
  294.5 11.7 %cholesky.50 = f32[128,128]{1,0:T(8,128)S(1)} custom-call(f32[128,128]{1,0:T(8,128)S(1)} %cholesky.118), custom_call_target="Cholesky" | custom-call | tf_op jit(solution)/shard_map/jit(cholesky)/cholesky | solution.py:15
  306.2 9.8 %custom-call.14 = f32[1,128,128]{1,2,0:T(8,128)S(1)} custom-call(f32[1,128,128]{2,1,0:T(8,128)S(1)} %get-tuple-element.28), custom_call_target="InvertDiagBlocksLowerTriangular" | custom-call | tf_op jit(solution)/shard_map/jit(cholesky)/cholesky | solution.py:15
  316.1 0.2 constant_dynamic-update-slice_fusion.1
  316.3 0.3 convolution_subtract_fusion.1
  316.5 11.7 %cholesky.105 = f32[128,128]{1,0:T(8,128)S(1)} custom-call(f32[128,128]{1,0:T(8,128)S(1)} %convolution_subtract_fusion.1), custom_call_target="Cholesky" | custom-call | tf_op jit(solution)/shard_map/jit(cholesky)/cholesky | solution.py:15
  328.3 0.6 compare_reduce_fusion
  330.3 4.0 while.1
  330.4 0.6 fusion.30
  330.9 1.4 bitcast_dynamic-update-slice_fusion.2
  332.4 0.6 fusion.30
  332.9 1.4 bitcast_dynamic-update-slice_fusion.2
  334.3 19.9 %custom-call.15 = f32[2,128,128]{1,2,0:T(8,128)S(1)} custom-call(f32[2,128,128]{2,1,0:T(8,128)S(1)} %get-tuple-element.11), custom_call_target="InvertDiagBlocksLowerTriangular" | custom-call | tf_op jit(solution)/shard_map/triangular_solve | solution.py:8
  354.3 3.8 fusion.19
  358.0 3.5 convolution_subtract_fusion
  361.6 2.0 convolution_convert_fusion
  363.6 1.5 fusion.7
  365.1 175.7 %all-reduce.6.cloned.1.call-done = bf16[256,256]{1,0:T(8,128)(2,1)} async-done(((bf16[256,256]{1,0:T(8,128)(2,1)}), bf16[256,256]{1,0:T(8,128)(2,1)}) %all-reduce.6.cloned.1.call-update) | async-done | bytes 131088 | tf_op jit(solution)/shard_map/psum | solution.py:26
  540.9 0.9 multiply_convert_fusion.1
  541.8 7.3 %multiply_convert_fusion = (bf16[4096,256]{1,0:T(8,128)(2,1)}, bf16[4096,256]{1,0:T(8,128)(2,1)}, bf16[1,4096,256]{2,1,0:T(8,128)(2,1)}) fusion(bf16[4096,256]{1,0:T(8,128)(2,1)} %param.6, bf16[1,4096,256]{2,1,0:T(8,128)(2,1)S(1)} %copy-done.2, bf16[1,4096,256]{2,1,0:T(8,128)(2,1)} %param.4, bf16[256,256]{1,0:T(8,128)(2,1)S(1)} %multiply_convert_fusion.1, ...), kind=kOutput, calls=%fused_computation.4 | convolution fusion | flops 556793856 | bytes 14811136 | tf_op jit(solution)/shard_map/dot_general | solution.py:28
  (26 shorter events, 0.4 us)
Async XLA Ops:
  7.2 0.9 copy-start
  7.2 277.0 %all-reduce.4.cloned.1.call-start = ((), (), s32[]{:S(2)}) async-start(), calls=%async_computation | async-start | bytes 8388608 | tf_op jit(solution)/shard_map/psum | solution.py:21
  13.0 527.8 %all-reduce.6.cloned.1.call-start = ((), (), s32[]{:S(2)}) async-start(), calls=%async_computation.1 | async-start | bytes 262144 | tf_op jit(solution)/shard_map/psum | solution.py:26
  354.2 3.8 copy-start.1
  358.0 5.6 %copy-start.4 = (bf16[4096,128]{0,1:T(8,128)(2,1)}, bf16[4096,128]{0,1:T(8,128)(2,1)S(1)}, u32[]{:S(2)}) copy-start(bf16[4096,128]{0,1:T(8,128)(2,1)S(1)} %get-tuple-element.31) | copy-start | bytes 3145732
  358.0 5.6 copy-start.3
  361.5 2.1 copy-start.2
  541.8 7.3 %copy-start.5 = (bf16[256,256]{1,0:T(8,128)(2,1)}, bf16[256,256]{1,0:T(8,128)(2,1)S(1)}, u32[]{:S(2)}) copy-start(bf16[256,256]{1,0:T(8,128)(2,1)S(1)} %multiply_convert_fusion.1) | copy-start | bytes 393220
Sparse Core Ops, SparseCore 0:
  13.5 270.6 all-reduce.3
  365.3 175.5 all-reduce.5
where the time goes:
time: 556 us
  waiting for transfers between devices  447 us (80%)
  other arithmetic  54.8 us (10%)
  matrix products  33.5 us (6%)
  between operations  15.5 us (3%)
    psum x1, waiting for transfers between devices, body(): left = lax.psum(term, ('outer', 'tp'))  271 us
    psum x1, waiting for transfers between devices, body(): lax.psum(local_right.astype(jnp.bfloat16), 'outer').astype(jnp.float32)  176 us
    another operation x6, other arithmetic, factor_whole(): return orthonormal(left, jnp.linalg.cholesky(gram))  34 us
    another operation x3, other arithmetic, orthonormal(): lax.linalg.triangular_solve(lower, left, left_side=False, lower=True, tra...  19.9 us
  transfers between devices with their start and end apart: 2, of which 2 were waited for; matrix products, arithmetic and copies ran while one was open for 0% of the time, Pallas kernels for 0%

commit v1 on v0

v1 whole, which is shorter than its diff:
```python
import jax
import jax.numpy as jnp
from jax import lax
from jax.experimental import pallas as pl
from jax.experimental.pallas import tpu as pltpu
from jax.sharding import PartitionSpec as P

MESH = pl.DeviceIdType.MESH
F32, BF16 = jnp.float32, jnp.bfloat16
NX, NY, NZ, ZLO = 4, 4, 8, 4
ROWS, RANK, HALF = 4096, 256, 128
MINE = ROWS // 2
PART = MINE // 2
LINE = PART // NX
SUB = LINE // NY
TILE = 16
PODS = 16
OWNERS = 2 * NX
PIECE = RANK // OWNERS


HIGH = lax.Precision.HIGHEST


def mm(a, b, dims):
    return lax.dot_general(a, b, (dims, ((), ())), precision=HIGH, preferred_element_type=F32)


def reciprocal(d):
    guess = pltpu.reciprocal(d, approx=True)
    guess = guess * (2.0 - d * guess)
    return guess * (2.0 - d * guess)


def factor_block(a, between):
    shape = (8, 128)
    lane = lax.broadcasted_iota(jnp.int32, shape, 1)
    row = lax.broadcasted_iota(jnp.int32, shape, 0)
    rest = a
    done = []
    for g in range(16):
        first = 8 * g
        pivots, rest = rest[:8], rest[8:]
        cols = jnp.stack([jnp.broadcast_to(pivots[:, first + c:first + c + 1], shape) for c in range(8)])
        here = (lane >= first) & (lane < first + 8)
        pivots = jnp.where(here, jnp.where(lane - first == row, 1.0, 0.0), pivots)
        upper = jnp.zeros(shape, F32)
        diag = jnp.ones(shape, F32)
        for p in range(0, 8, 2):
            q = p + 1
            at_p, at_q = row == p, row == q
            either = at_p | at_q
            col_p, col_q, cols = cols[0], cols[1], cols[2:]
            d_p = jnp.broadcast_to(col_p[p:p + 1], shape)
            d_pq = jnp.broadcast_to(col_p[q:q + 1], shape)
            d_q = jnp.broadcast_to(col_q[q:q + 1], shape)
            det = d_p * d_q - d_pq * d_pq
            inv = reciprocal(det)
            line_p = jnp.broadcast_to(pivots[p:p + 1], shape)
            line_q = jnp.broadcast_to(pivots[q:q + 1], shape)
            new_p = d_q * line_p - d_pq * line_q
            new_q = d_p * line_q - d_pq * line_p
            over = reciprocal(d_p)
            upper = jnp.where(at_p, pivots, jnp.where(at_q, new_q * over, upper))
            diag = jnp.where(at_p, d_p, jnp.where(at_q, det * over, diag))
            change = jnp.where(at_p, new_p, jnp.where(at_q, new_q, -(col_p * new_p + col_q * new_q)))
            pivots = jnp.where(either, 0.0, pivots) + change * inv
            if p < 6:
                full = cols.shape
                edge_p = jnp.broadcast_to(cols[:, p:p + 1], full)
                edge_q = jnp.broadcast_to(cols[:, q:q + 1], full)
                new_p = d_q[None] * edge_p - d_pq[None] * edge_q
                new_q = d_p[None] * edge_q - d_pq[None] * edge_p
                other = -(col_p[None] * new_p + col_q[None] * new_q)
                change = jnp.where(at_p[None], new_p, jnp.where(at_q[None], new_q, other))
                cols = jnp.where(either[None], 0.0, cols) + change * inv[None]
        done.append(jnp.where(lane <= row + first, upper * (1.0 / jnp.sqrt(diag)), 0.0))
        if g < 15:
            total = jnp.where(here[:1], 0.0, rest)
            for c in range(8):
                total = total - rest[:, first + c:first + c + 1] * pivots[c:c + 1]
            rest = total
        if g in between:
            between[g]()
    return jnp.concatenate(done, axis=0)


def inverse_factor(gram, between):
    on = lax.broadcasted_iota(jnp.int32, gram.shape, 0) == lax.broadcasted_iota(jnp.int32, gram.shape, 1)
    diagonal = jnp.where(on, gram, 0.0)
    scale = 1.0 / jnp.sqrt(jnp.sum(diagonal, axis=0, keepdims=True))
    gram = gram * scale * (1.0 / jnp.sqrt(jnp.sum(diagonal, axis=1, keepdims=True)))
    w11 = factor_block(gram[:128, :128], between[0])
    l21 = mm(gram[128:, :128], w11, ((1,), (1,)))
    w22 = factor_block(gram[128:, 128:] - mm(l21, l21, ((1,), (1,))), between[1])
    w21 = -mm(w22, mm(l21, w11, ((1,), (0,))), ((1,), (0,)))
    top = jnp.concatenate([w11, jnp.zeros((128, 128), F32)], axis=1)
    return jnp.concatenate([top, jnp.concatenate([w21, w22], axis=1)], axis=0) * scale


def device(x, y, z, core):
    return ((z // ZLO) * NX + x) * 2 + core, (z % ZLO) * NY + y


def send(src, dst, send_sem, recv_sem, dev):
    return pltpu.make_async_remote_copy(
        src_ref=src, dst_ref=dst, send_sem=send_sem, recv_sem=recv_sem, device_id=dev, device_id_type=MESH
    )


def exchange(
    delta, error, momentum, q_in, left, merged, held, high, low, new_factor,
    q, dbuf, ebuf, pair_in, pair, s1, keep, r1o, r1d, r1p, o1, s2, r2, s3, r3, o3, g3,
    gpart, gsum, gin, zsum, zsend, zr, zown, zpair, zall,
    ld, cs, cr, p1s, p1r, p2s, p2r, p3s, p3r, a3s, a3r, a2s, a2r, a1s, a1r, axs, axr, acs, acr,
    gs, gr, z1s, z1r, zps, zpr, z2s, z2r,
):
    o, t = lax.axis_index("outer"), lax.axis_index("tp")
    core, x, y = lax.rem(o, 2), lax.rem(o // 2, NX), lax.rem(t, NY)
    z = (o // (2 * NX)) * ZLO + t // NY
    sibling = device(x, y, z, 1 - core)
    c1, c2 = (x, y), (y, x)

    def peer1(h, v):
        return device(v, y, z, core) if h == 0 else device(x, v, z, core)

    def peer2(h, v):
        return device(x, v, z, core) if h == 0 else device(v, y, z, core)

    def turn(v, i, n):
        return lax.rem(v + i, n)

    def rows(start, size):
        return pl.ds(pl.multiple_of(start, TILE), size)

    mine, theirs = core * MINE, (1 - core) * MINE

    def line(h, i):
        return h * PART + turn(c1[h], i, NX) * LINE

    order = [(i, h) for i in (2, 1, 3, 0) for h in range(2)]

    def loads(k, base, i, h):
        src = rows(base + line(h, i), LINE)
        return (
            pltpu.make_async_copy(delta.at[0, src], dbuf.at[src], ld.at[k, 0]),
            pltpu.make_async_copy(error.at[0, src], ebuf.at[src], ld.at[k, 1]),
        )

    barrier = pltpu.get_barrier_semaphore()
    greeted = [sibling]
    greeted += [device(turn(x, i, NX), y, z, core) for i in range(1, NX)]
    greeted += [device(x, turn(y, i, NY), z, core) for i in range(1, NY)]
    greeted += [device(x, y, turn(z, i, NZ), core) for i in range(1, NZ)]
    greeted += [device(turn(x, i, NX), y, z, 1 - core) for i in range(1, NX)]
    for dev in greeted:
        pl.semaphore_signal(barrier, inc=1, device_id=dev, device_id_type=MESH)

    steps = [loads(k, theirs, i, h) for k, (i, h) in enumerate(order)]
    steps += [loads(8 + k, mine, i, h) for k, (i, h) in enumerate(order)]
    for step in steps:
        for copy in step:
            copy.start()
    load_q = pltpu.make_async_copy(q_in, q, ld.at[16, 0])
    load_q.start()

    pending = []

    def go(*args):
        copy = send(*args)
        copy.start()
        pending.append(copy)

    def merge(k, base, i, h):
        for copy in steps[k]:
            copy.wait()
        block = rows(base + line(h, i), LINE)
        total = (dbuf[block, :].astype(F32) + ebuf[block, :].astype(F32)).astype(BF16)
        merged[block, :] = total
        return block, total

    for k, (i, h) in enumerate(order):
        block, _ = merge(k, theirs, i, h)
        if k == 0:
            pl.semaphore_wait(barrier, len(greeted))
        here = rows(line(h, i), LINE)
        go(merged.at[block], pair_in.at[here], cs.at[h, i], cr.at[h, i], sibling)
    load_q.wait()

    half = LINE // 2

    def up(h):
        return peer1(h, turn(c1[h], 1, NX))

    def down(h):
        return peer1(h, turn(c1[h], NX - 1, NX))

    for k, (i, h) in enumerate(order):
        _, total = merge(8 + k, mine, i, h)
        at = line(h, i)
        here = rows(at, LINE)
        send(pair_in.at[here], pair_in.at[here], cs.at[h, i], cr.at[h, i], sibling).wait_recv()
        both = (total.astype(F32) + pair_in[here, :].astype(F32)).astype(BF16)
        pair[here, :] = both
        term = jnp.dot(both, q[...], preferred_element_type=F32)
        first, second = rows(at, half), rows(at + half, half)
        if i == 2:
            s1[here, :] = term.astype(BF16)
            go(s1.at[first], r1d.at[h, 0], p1s.at[h, 0, 0], p1r.at[h, 0, 0], up(h))
            go(s1.at[second], r1d.at[h, 1], p1s.at[h, 1, 0], p1r.at[h, 1, 0], down(h))
        elif i == 1:
            s1[second, :] = term[half:].astype(BF16)
            go(s1.at[second], r1o.at[h, 0], p1s.at[h, 0, 1], p1r.at[h, 0, 1], up(h))
            keep[h, 0] = term[:half]
        elif i == 3:
            s1[first, :] = term[:half].astype(BF16)
            go(s1.at[first], r1o.at[h, 1], p1s.at[h, 1, 1], p1r.at[h, 1, 1], down(h))
            keep[h, 1] = term[half:]
        else:
            o1[h] = term
    for h in range(2):
        send(r1d.at[h, 0], r1d.at[h, 0], p1s.at[h, 0, 0], p1r.at[h, 0, 0], down(h)).wait_recv()
        first = rows(line(h, 1), half)
        s1[first, :] = (keep[h, 0] + r1d[h, 0].astype(F32)).astype(BF16)
        go(s1.at[first], r1p.at[h, 0], p1s.at[h, 0, 2], p1r.at[h, 0, 2], up(h))
        send(r1d.at[h, 1], r1d.at[h, 1], p1s.at[h, 1, 0], p1r.at[h, 1, 0], up(h)).wait_recv()
        second = rows(line(h, 3) + half, half)
        s1[second, :] = (keep[h, 1] + r1d[h, 1].astype(F32)).astype(BF16)
        go(s1.at[second], r1p.at[h, 1], p1s.at[h, 1, 2], p1r.at[h, 1, 2], down(h))

    load_momentum = pltpu.make_async_copy(momentum, held, ld.at[16, 1])
    load_momentum.start()

    for h in range(2):
        send(r1o.at[h, 0], r1o.at[h, 0], p1s.at[h, 0, 1], p1r.at[h, 0, 1], down(h)).wait_recv()
        send(r1o.at[h, 1], r1o.at[h, 1], p1s.at[h, 1, 1], p1r.at[h, 1, 1], up(h)).wait_recv()
        send(r1p.at[h, 0], r1p.at[h, 0], p1s.at[h, 0, 2], p1r.at[h, 0, 2], down(h)).wait_recv()
        send(r1p.at[h, 1], r1p.at[h, 1], p1s.at[h, 1, 2], p1r.at[h, 1, 2], up(h)).wait_recv()
        o1[h, :half] += r1p[h, 0].astype(F32) + r1o[h, 1].astype(F32)
        o1[h, half:] += r1o[h, 0].astype(F32) + r1p[h, 1].astype(F32)
        s2[h] = o1[h].astype(BF16)
        for i in (2, 1, 3):
            b = turn(c2[h], i, NY)
            go(s2.at[h, rows(b * SUB, SUB)], r2.at[h, c2[h]], p2s.at[h, b], p2r.at[h, c2[h]], peer2(h, b))
    for h in range(2):
        for i in range(1, NY):
            b = turn(c2[h], i, NY)
            send(r2.at[h, b], r2.at[h, b], p2s.at[h, b], p2r.at[h, b], peer2(h, b)).wait_recv()
        total = o1[h, rows(c2[h] * SUB, SUB), :]
        for i in range(1, NY):
            total += r2[h, turn(c2[h], i, NY)].astype(F32)
        for c in range(2):
            o3[h, c] = total[:, c * HALF:(c + 1) * HALF]
            s3[h, c] = total[:, c * HALF:(c + 1) * HALF].astype(BF16)

    far = (4, 3, 5, 2, 6, 1, 7)

    def spot(v):
        return v // 4, rows((v % 4) * TILE, TILE)

    for i in far:
        b = turn(z, i, NZ)
        c, at = spot(b)
        go(s3.at[:, c, at], r3.at[z], p3s.at[b], p3r.at[z], device(x, y, b, core))
    for i in far:
        b = turn(z, i, NZ)
        send(r3.at[b], r3.at[b], p3s.at[b], p3r.at[b], device(x, y, b, core)).wait_recv()

    def sub(h, i, j):
        return rows(mine + line(h, i) + turn(c2[h], j, NY) * SUB, SUB)

    c, at = spot(z)
    for h in range(2):
        total = o3[h, c, at, :]
        for i in range(1, NZ):
            total += r3[turn(z, i, NZ), h].astype(F32)
        g3[z, h] = total.astype(BF16)
    for i in far:
        b = turn(z, i, NZ)
        go(g3.at[z], g3.at[z], a3s.at[b], a3r.at[z], device(x, y, b, core))

    def along(h, j):
        at, b = left.at[sub(h, 0, j)], turn(c2[h], j, NY)
        go(at, at, a1s.at[h, 0, b], a1r.at[h, 0, b], up(h))
        go(at, at, a1s.at[h, 1, b], a1r.at[h, 1, b], down(h))

    def arrive(h, side, j):
        at, b = left.at[sub(h, 3 if side == 0 else 1, j)], turn(c2[h], j, NY)
        send(at, at, a1s.at[h, side, b], a1r.at[h, side, b], down(h) if side == 0 else up(h)).wait_recv()

    def relay(h, side, j):
        at, b = left.at[sub(h, 3 if side == 0 else 1, j)], turn(c2[h], j, NY)
        go(at, at, axs.at[h, b], axr.at[h, b], up(h) if side == 0 else down(h))

    def cross(h, i):
        at = left.at[rows(mine + line(h, i), LINE)]
        go(at, at, acs.at[h, i], acr.at[h, i], sibling)

    zsum[...] = jnp.zeros_like(zsum)

    def products(h, i):
        within = line(h, i)
        part = left[rows(mine + within, LINE), :]
        both = jnp.concatenate([part, pair[rows(within, LINE), :]], axis=1)
        product = lax.dot_general(part, both, (((0,), (0,)), ((), ())), preferred_element_type=F32)
        gpart[h * NX + turn(c1[h], i, NX)] = product[:, :RANK]
        zsum[...] += product[:, RANK:]

    for i in far:
        b = turn(z, i, NZ)
        send(g3.at[b], g3.at[b], a3s.at[b], a3r.at[b], device(x, y, b, core)).wait_recv()
    for h in range(2):
        left[sub(h, 0, 0), :] = jnp.concatenate(
            [jnp.concatenate([g3[c * 4 + v, h] for c in range(2)], axis=1) for v in range(4)], axis=0
        )
        at = left.at[sub(h, 0, 0)]
        for i in (2, 1, 3):
            b = turn(c2[h], i, NY)
            go(at, at, a2s.at[h, b], a2r.at[h, c2[h]], peer2(h, b))
        along(h, 0)
    for j in (1, 3, 2):
        for h in range(2):
            at, b = left.at[sub(h, 0, j)], turn(c2[h], j, NY)
            send(at, at, a2s.at[h, b], a2r.at[h, b], peer2(h, b)).wait_recv()
            along(h, j)
    for h in range(2):
        arrive(h, 0, 0)
        relay(h, 0, 0)
    products(0, 0)
    for j, side in ((1, 0), (3, 1)):
        for h in range(2):
            arrive(h, side, j)
            relay(h, side, j)
    products(1, 0)
    for h in range(2):
        arrive(h, 1, 2)
        relay(h, 1, 2)
        cross(h, 0)
    for h in range(2):
        arrive(h, 0, 3)
        arrive(h, 0, 2)
        cross(h, 3)
        products(h, 3)
    for h in range(2):
        arrive(h, 1, 0)
        arrive(h, 1, 1)
        cross(h, 1)
        products(h, 1)
    for h in range(2):
        for j in (0, 1, 3, 2):
            at, b = left.at[sub(h, 2, j)], turn(c2[h], j, NY)
            dev = down(h) if j < 2 else up(h)
            send(at, at, axs.at[h, b], axr.at[h, b], dev).wait_recv()
        products(h, 2)

    total = gpart[0]
    for i in range(1, 2 * NX):
        total += gpart[i]
    gsum[...] = total
    go(gsum, gin, gs.at[0], gr.at[0], sibling)

    owner = x * 2 + core
    others = [(turn(x, i, NX), lax.rem(core + e, 2)) for i in range(NX) for e in range(2) if i or e]

    def piece(v, c):
        return rows((v * 2 + c) * PIECE, PIECE)

    zsend[...] = zsum[...].astype(BF16)
    for v, c in others:
        go(zsend.at[piece(v, c)], zr.at[owner], z1s.at[v * 2 + c], z1r.at[owner], device(v, y, z, c))
    for h in range(2):
        cross(h, 2)
    across = device(x, y, turn(z, ZLO, NZ), core)

    def add_pieces():
        for v, c in others:
            e = v * 2 + c
            send(zr.at[e], zr.at[e], z1s.at[e], z1r.at[e], device(v, y, z, c)).wait_recv()
        total = zsum[piece(x, core), :]
        for v, c in others:
            total += zr[v * 2 + c].astype(F32)
        zown[...] = total.astype(BF16)
        go(zown, zpair, zps.at[0], zpr.at[0], across)

    def add_across():
        send(zpair, zpair, zps.at[0], zpr.at[0], across).wait_recv()
        here = piece(x, core)
        zall[here, :] = (zown[...].astype(F32) + zpair[...].astype(F32)).astype(BF16)
        for v, c in others:
            go(zall.at[here], zall.at[here], z2s.at[v * 2 + c], z2r.at[owner], device(v, y, z, c))

    send(gin, gin, gs.at[0], gr.at[0], sibling).wait_recv()
    inverse = inverse_factor(gsum[...] + gin[...], ({12: add_pieces}, {8: add_across}))
    for v, c in others:
        e = v * 2 + c
        send(zall.at[piece(v, c)], zall.at[piece(v, c)], z2s.at[e], z2r.at[e], device(v, y, z, c)).wait_recv()
    factor = (mm(inverse, zall[...].astype(F32), ((1,), (0,))) / PODS).astype(BF16)
    new_factor[...] = factor.T
    mix = mm(inverse, factor.astype(F32), ((0,), (0,)))
    head = mix.astype(BF16)
    high[...] = head
    low[...] = (mix - head.astype(F32)).astype(BF16)

    for h in range(2):
        for i in range(NX):
            at = left.at[rows(theirs + line(h, i), LINE)]
            send(at, at, acs.at[h, i], acr.at[h, i], sibling).wait_recv()
    load_momentum.wait()
    for copy in pending:
        copy.wait_send()


def gather(delta, error, momentum, q):
    vmem, hbm = (pl.BlockSpec(memory_space=s) for s in (pltpu.VMEM, pltpu.HBM))
    dma = pltpu.SemaphoreType.DMA
    wide, square = (ROWS, RANK), (RANK, RANK)
    return pl.pallas_call(
        exchange,
        out_shape=(
            jax.ShapeDtypeStruct(wide, BF16),
            jax.ShapeDtypeStruct(wide, BF16),
            jax.ShapeDtypeStruct(wide, BF16),
            jax.ShapeDtypeStruct(square, BF16),
            jax.ShapeDtypeStruct(square, BF16),
            jax.ShapeDtypeStruct(square, BF16),
        ),
        in_specs=[hbm] * 4,
        out_specs=(vmem,) * 6,
        scratch_shapes=[
            pltpu.VMEM(square, BF16),
            pltpu.VMEM(wide, BF16),
            pltpu.VMEM(wide, BF16),
            pltpu.VMEM((MINE, RANK), BF16),
            pltpu.VMEM((MINE, RANK), BF16),
            pltpu.VMEM((MINE, RANK), BF16),
            pltpu.VMEM((2, 2, LINE // 2, RANK), F32),
            pltpu.VMEM((2, 2, LINE // 2, RANK), BF16),
            pltpu.VMEM((2, 2, LINE // 2, RANK), BF16),
            pltpu.VMEM((2, 2, LINE // 2, RANK), BF16),
            pltpu.VMEM((2, LINE, RANK), F32),
            pltpu.VMEM((2, LINE, RANK), BF16),
            pltpu.VMEM((2, NY, SUB, RANK), BF16),
            pltpu.VMEM((2, 2, SUB, HALF), BF16),
            pltpu.VMEM((NZ, 2, TILE, HALF), BF16),
            pltpu.VMEM((2, 2, SUB, HALF), F32),
            pltpu.VMEM((NZ, 2, TILE, HALF), BF16),
            pltpu.VMEM((2 * NX,) + square, F32),
            pltpu.VMEM(square, F32),
            pltpu.VMEM(square, F32),
            pltpu.VMEM(square, F32),
            pltpu.VMEM(square, BF16),
            pltpu.VMEM((OWNERS, PIECE, RANK), BF16),
            pltpu.VMEM((PIECE, RANK), BF16),
            pltpu.VMEM((PIECE, RANK), BF16),
            pltpu.VMEM(square, BF16),
            dma((17, 2)),
            dma((2, NX)), dma((2, NX)),
            dma((2, 2, 3)), dma((2, 2, 3)),
            dma((2, NY)), dma((2, NY)),
            dma((NZ,)), dma((NZ,)),
            dma((NZ,)), dma((NZ,)),
            dma((2, NY)), dma((2, NY)),
            dma((2, 2, NY)), dma((2, 2, NY)),
            dma((2, NY)), dma((2, NY)),
            dma((2, NX)), dma((2, NX)),
            dma((1,)), dma((1,)),
            dma((OWNERS,)), dma((OWNERS,)),
            dma((1,)), dma((1,)),
            dma((OWNERS,)), dma((OWNERS,)),
        ],
        compiler_params=pltpu.CompilerParams(collective_id=0, has_side_effects=True, vmem_limit_bytes=32 << 20),
        cost_estimate=pl.CostEstimate(flops=6 * ROWS * RANK * RANK, bytes_accessed=5 * ROWS * RANK * 2, transcendentals=0),
        name="gather_left",
    )(*(pltpu.with_memory_space_constraint(a, pltpu.HBM) for a in (delta, error, momentum, q)))


def finish(left, merged, momentum, high, low, factor, new_error, new_momentum, outer_step, new_factor, e, m, s, sem):
    size, count = ROWS // 8, 8
    copies = [pltpu.make_async_copy(factor, new_factor, sem.at[count, 0])]
    copies[0].start()
    for i in range(count):
        at = pl.ds(i * size, size)
        block = left[at, :]
        approx = jnp.dot(block, high[...], preferred_element_type=F32) + jnp.dot(
            block, low[...], preferred_element_type=F32
        )
        e[at, :] = (merged[at, :].astype(F32) - approx).astype(BF16)
        moment = 0.9 * momentum[at, :].astype(F32) + approx
        m[at, :] = moment.astype(BF16)
        s[at, :] = (0.7 * (approx + 0.9 * moment)).astype(BF16)
        for k, (src, dst) in enumerate(((e, new_error.at[0, at]), (m, new_momentum.at[at]), (s, outer_step.at[at]))):
            copies.append(pltpu.make_async_copy(src.at[at], dst, sem.at[i, k]))
            copies[-1].start()
    for copy in copies:
        copy.wait()


def outputs(left, merged, momentum, high, low, factor):
    any_, vmem = pl.BlockSpec(memory_space=pl.ANY), pl.BlockSpec(memory_space=pltpu.VMEM)
    wide = (ROWS, RANK)
    return pl.pallas_call(
        finish,
        out_shape=(
            jax.ShapeDtypeStruct((1,) + wide, BF16),
            jax.ShapeDtypeStruct(wide, BF16),
            jax.ShapeDtypeStruct(wide, BF16),
            jax.ShapeDtypeStruct((RANK, RANK), BF16),
        ),
        in_specs=[vmem] * 6,
        out_specs=(any_,) * 4,
        scratch_shapes=[pltpu.VMEM(wide, BF16)] * 3 + [pltpu.SemaphoreType.DMA((9, 3))],
        compiler_params=pltpu.CompilerParams(vmem_limit_bytes=24 << 20),
        cost_estimate=pl.CostEstimate(flops=4 * ROWS * RANK * RANK, bytes_accessed=6 * ROWS * RANK * 2, transcendentals=0),
        name="outputs",
    )(left, merged, momentum, high, low, factor)


def body(delta, error, momentum, q_init):
    left, merged, held, high, low, factor = gather(delta, error, momentum, q_init)
    return outputs(left, merged, held, high, low, factor)


def solution(mesh):
    placed = (P("outer", None, "tp"), P("outer", None, "tp"), P(None, "tp"), P("tp", None))
    return jax.shard_map(
        body,
        mesh=mesh,
        in_specs=placed,
        out_specs=(P("outer", None, "tp"), P(None, "tp"), P(None, "tp"), P("tp", None)),
        check_vma=False,
    )
```

time: 556 us -> 68.8 us (0.12)
  waiting for transfers between devices: 447 us -> 0 us
  Pallas kernels: 0 us -> 68.1 us
  other arithmetic: 54.8 us -> 0 us
  matrix products: 33.5 us -> 0 us
  between operations: 15.5 us -> 0.64 us
    psum x2 -> x0, waiting for transfers between devices: 447 us -> none  [the longest x1 271 us: body(): left = lax.psum(term, ('outer', 'tp'))]
    pallas_call x0 -> x2, Pallas kernels: none -> 68.1 us  [the longest x1 64.6 us: gather(): pl.pallas_call(exchange, out_shape=(jax.ShapeDtypeStruct(wide, BF16), jax...]
    another operation x9 -> x0, other arithmetic: 53.9 us -> none  [the longest x6 34 us: factor_whole(): return orthonormal(left, jnp.linalg.cholesky(gram))]
    dot_general x4 -> x0, matrix products: 23.7 us -> none  [the longest x1 10.1 us: factor_whole(): gram = jnp.dot(left.T, left, precision=lax.Precision.HIGHEST)]
    another operation x5 -> x0, matrix products: 9.73 us -> none  [the longest x3 9.25 us: orthonormal(): lax.linalg.triangular_solve(lower, left, left_side=False, lower=True, tra...]
  transfers between devices with their start and end apart: 2 -> 0, of which waited for: 2 -> 0; matrix products, arithmetic and copies ran while one was open for 0% -> 0% of each run, Pallas kernels for 0% -> 0%
where the time goes in v1:
time: 68.8 us
  Pallas kernels  68.1 us (99%)
    pallas_call x1, Pallas kernels, gather(): pl.pallas_call(exchange, out_shape=(jax.ShapeDtypeStruct(wide, BF16), jax...  64.6 us
    pallas_call x1, Pallas kernels, outputs(): pl.pallas_call(finish, out_shape=(jax.ShapeDtypeStruct((1,) + wide, BF16)...  3.47 us

profile of v1, /device:TPU:1, one launch (start us, length us, event | category | flops | bytes accessed | tf_op | source)
XLA Modules:
  0.0 68.8 jit_solution(1787945819000337083)
XLA Ops:
  0.6 64.6 %gather_left.1 = (bf16[4096,256]{1,0:T(8,128)(2,1)S(1)}, bf16[4096,256]{1,0:T(8,128)(2,1)S(1)}, bf16[4096,256]{1,0:T(8,128)(2,1)S(1)}, bf16[256,256]{1,0:T(8,128...) custom-call(bf16[1,4096,256]{2,1,0:T(8,128)(2,1)} %delta.1, bf16[1,4096,256]{2,1,0:T(8,128)(2,1)} %error.1, ...), custom_call_target="tpu_custom_call" | custom-call | flops 1610612736 | bytes 10485760 | tf_op jit(solution)/shard_map/gather_left/pallas_call | solution.py:417
  65.3 3.5 %outputs.1 = (bf16[1,4096,256]{2,1,0:T(8,128)(2,1)}, bf16[4096,256]{1,0:T(8,128)(2,1)}, bf16[4096,256]{1,0:T(8,128)(2,1)}, bf16[256,256]{1,0:T(8,128)(2,1)}) custom-call(bf16[4096,256]{1,0:T(8,128)(2,1)S(1)} %get-tuple-element.10.left, bf16[4096,256]{1,0:T(8,128)(2,1)S(1)} %get-tuple-element.11.merged, bf16[4096,256]{1,0:T(8,128)(2,1)S(1)} %get-tuple-element.12.momentum, ...), custom_call_target="tpu_custom_call" | custom-call | flops 1073741824 | bytes 12582912 | tf_op jit(solution)/shard_map/outputs/pallas_call | solution.py:501

commit v2 on v1

v2 whole, which is shorter than its diff:
```python
import jax
import jax.numpy as jnp
from jax import lax
from jax.experimental import pallas as pl
from jax.experimental.pallas import tpu as pltpu
from jax.sharding import PartitionSpec as P

MESH = pl.DeviceIdType.MESH
F32, BF16 = jnp.float32, jnp.bfloat16
NX, NY, NZ, ZLO = 4, 4, 8, 4
ROWS, RANK, HALF = 4096, 256, 128
MINE = ROWS // 2
PART = MINE // 2
LINE = PART // NX
SUB = LINE // NY
TILE = 16
PODS = 16
OWNERS = 2 * NX
PIECE = RANK // OWNERS


HIGH = lax.Precision.HIGHEST


def mm(a, b, dims):
    return lax.dot_general(a, b, (dims, ((), ())), precision=HIGH, preferred_element_type=F32)


def reciprocal(d):
    return pltpu.reciprocal(d, approx=True)


def factor_block(a, between):
    tile = (8, 128)
    lane = lax.broadcasted_iota(jnp.int32, tile, 1)
    row = lax.broadcasted_iota(jnp.int32, tile, 0)
    tiles = a.reshape(16, 8, 128)
    both, rest = tiles[:2], tiles[2:]
    done = []
    for g in range(16):
        first = 8 * g
        shape = both.shape
        below = shape[0] - 1
        cols = [jnp.broadcast_to(both[:, :, first + c:first + c + 1], shape) for c in range(8)]
        here = (lane >= first) & (lane < first + 8)
        start = [jnp.where(here, jnp.where(lane - first == row, 1.0, 0.0), both[0])]
        start += [jnp.where(here, 0.0, both[1])] * below
        both = jnp.stack(start)
        diag = jnp.ones(tile, F32)

        def spread(x, r):
            return jnp.broadcast_to(x[0, r:r + 1], tile)

        def after(r, x):
            top = jnp.where(row > r, x[:1], 0.0)
            return jnp.concatenate([top, x[1:]], axis=0) if below else top

        for p in range(0, 8, 2):
            q = p + 1
            d_p, d_pq, d_q = spread(cols[p], p), spread(cols[p], q), spread(cols[q], q)
            det = d_p * d_q - d_pq * d_pq
            inv_p = reciprocal(d_p)
            inv_q = d_p * reciprocal(det)
            ratio = d_pq * inv_p
            line_p = spread(both, p)
            line_q = spread(both, q) - ratio * line_p
            diag = jnp.where(row == p, d_p, jnp.where(row == q, det * inv_p, diag))
            part_p = after(p, cols[p] * inv_p)
            part_q = after(q, (cols[q] - part_p * d_pq) * inv_q)
            both = both - part_p * line_p - part_q * line_q
            for k in range(q + 1, 8):
                edge_p = spread(cols[k], p)
                edge_q = spread(cols[k], q) - ratio * edge_p
                cols[k] = cols[k] - part_p * edge_p - part_q * edge_q
        upper = both[0]
        done.append(jnp.where(lane <= row + first, upper * (1.0 / jnp.sqrt(diag)), 0.0))
        if g < 14:
            factors = (upper / diag).T[first + 16:].reshape(rest.shape[0], 8, 8)
            rest = jnp.where(here, 0.0, rest)
            for c in range(8):
                rest = rest - factors[:, :, c:c + 1] * upper[c:c + 1]
            both = jnp.concatenate([both[1:], rest[:1]], axis=0)
            rest = rest[1:] if g < 13 else None
        elif g < 15:
            both = both[1:]
        if g in between:
            between[g]()
    return jnp.concatenate(done, axis=0)


def inverse_factor(gram, between):
    on = lax.broadcasted_iota(jnp.int32, gram.shape, 0) == lax.broadcasted_iota(jnp.int32, gram.shape, 1)
    diagonal = jnp.where(on, gram, 0.0)
    scale = 1.0 / jnp.sqrt(jnp.sum(diagonal, axis=0, keepdims=True))
    gram = gram * scale * (1.0 / jnp.sqrt(jnp.sum(diagonal, axis=1, keepdims=True)))
    w11 = factor_block(gram[:128, :128], between[0])
    l21 = mm(gram[128:, :128], w11, ((1,), (1,)))
    w22 = factor_block(gram[128:, 128:] - mm(l21, l21, ((1,), (1,))), between[1])
    w21 = -mm(w22, mm(l21, w11, ((1,), (0,))), ((1,), (0,)))
    top = jnp.concatenate([w11, jnp.zeros((128, 128), F32)], axis=1)
    return jnp.concatenate([top, jnp.concatenate([w21, w22], axis=1)], axis=0) * scale


def device(x, y, z, core):
    return ((z // ZLO) * NX + x) * 2 + core, (z % ZLO) * NY + y


def send(src, dst, send_sem, recv_sem, dev):
    return pltpu.make_async_remote_copy(
        src_ref=src, dst_ref=dst, send_sem=send_sem, recv_sem=recv_sem, device_id=dev, device_id_type=MESH
    )


def exchange(
    delta, error, momentum, q_in, left, merged, held, high, low, new_factor,
    q, dbuf, ebuf, pair_in, s1, xs, rx, sx, keep, r1o, r1d, r1p, o1, s2, r2, s3, r3, o3, g3,
    gpart, gsum, gin, zsum, zsend, zr, zown, zpair, zall,
    ld, ss, cr, p1d, p1r, p2r, oner, a2r, a1r, axr,
):
    o, t = lax.axis_index("outer"), lax.axis_index("tp")
    core, x, y = lax.rem(o, 2), lax.rem(o // 2, NX), lax.rem(t, NY)
    z = (o // (2 * NX)) * ZLO + t // NY
    sibling = device(x, y, z, 1 - core)
    c1, c2 = (x, y), (y, x)

    def peer1(h, v):
        return device(v, y, z, core) if h == 0 else device(x, v, z, core)

    def peer2(h, v):
        return device(x, v, z, core) if h == 0 else device(v, y, z, core)

    def turn(v, i, n):
        return lax.rem(v + i, n)

    def rows(start, size):
        return pl.ds(pl.multiple_of(start, TILE), size)

    mine, theirs = core * MINE, (1 - core) * MINE

    def line(h, i):
        return h * PART + turn(c1[h], i, NX) * LINE

    order = [(whose, i) for whose in range(2) for i in (2, 1, 3, 0)]

    def loads(whose, i, h):
        src, k = rows((mine if whose else theirs) + line(h, i), LINE), whose * NX + i
        return (
            pltpu.make_async_copy(delta.at[0, src], dbuf.at[src], ld.at[k]),
            pltpu.make_async_copy(error.at[0, src], ebuf.at[src], ld.at[k]),
        )

    barrier = pltpu.get_barrier_semaphore()
    greeted = [sibling]
    greeted += [device(turn(x, i, NX), y, z, core) for i in range(1, NX)]
    greeted += [device(x, turn(y, i, NY), z, core) for i in range(1, NY)]
    greeted += [device(x, y, turn(z, i, NZ), core) for i in range(1, NZ)]
    greeted += [device(turn(x, i, NX), y, z, 1 - core) for i in range(1, NX)]
    for dev in greeted:
        pl.semaphore_signal(barrier, inc=1, device_id=dev, device_id_type=MESH)

    for whose, i in order:
        for h in range(2):
            for copy in loads(whose, i, h):
                copy.start()
    load_q = pltpu.make_async_copy(q_in, q, ld.at[8])
    load_q.start()

    stages = ("core", "first", "second", "z", "merged", "tiles", "gather", "lines", "cross", "gram", "right", "across", "back")

    def go(stage, src, dst, recv_sem, dev):
        send(src, dst, ss.at[stages.index(stage)], recv_sem, dev).start()

    def sent(stage, ref):
        sem = ss.at[stages.index(stage)]
        send(ref, ref, sem, sem, sibling).wait_send()

    def landed(ref, sem):
        send(ref, ref, ss.at[0], sem, sibling).wait_recv()

    def span(ref, size):
        return ref.at[pl.ds(0, size)]

    def merge(whose, i, h):
        if h == 0:
            every = span(dbuf, 4 * LINE)
            pltpu.make_async_copy(every, every, ld.at[whose * NX + i]).wait()
        block = rows((mine if whose else theirs) + line(h, i), LINE)
        total = (dbuf[block, :].astype(F32) + ebuf[block, :].astype(F32)).astype(BF16)
        merged[block, :] = total
        return block, total.astype(F32)

    half = LINE // 2

    def up(h):
        return peer1(h, turn(c1[h], 1, NX))

    def down(h):
        return peer1(h, turn(c1[h], NX - 1, NX))

    def give(i, h):
        block, _ = merge(0, i, h)
        here = rows(line(h, i), LINE)
        go("core", merged.at[block], pair_in.at[here], cr.at[i], sibling)

    def take(i, h):
        _, total = merge(1, i, h)
        at = line(h, i)
        here = rows(at, LINE)
        if h == 0:
            landed(span(pair_in, 2 * LINE), cr.at[i])
        total = total + pair_in[here, :].astype(F32)
        if h == 1:
            both = total.astype(BF16)
            xs[turn(y, i, NY)] = both.reshape(NX, SUB, RANK)
            total = jnp.dot(both, q[...], preferred_element_type=F32)
        first, second = rows(at, half), rows(at + half, half)
        if i == 2:
            s1[here, :] = total.astype(BF16)
            go("first", s1.at[first], r1d.at[h, 0], p1d.at[h, 0], up(h))
            go("first", s1.at[second], r1d.at[h, 1], p1d.at[h, 1], down(h))
        elif i == 1:
            s1[second, :] = total[half:].astype(BF16)
            go("first", s1.at[second], r1o.at[h, 0], p1r.at[h], up(h))
            keep[h, 0] = total[:half]
        elif i == 3:
            s1[first, :] = total[:half].astype(BF16)
            go("first", s1.at[first], r1o.at[h, 1], p1r.at[h], down(h))
            keep[h, 1] = total[half:]
        else:
            o1[h] = total

    for n, (whose, i) in enumerate(order):
        if n == 0:
            pl.semaphore_wait(barrier, len(greeted))
        if n == 2:
            load_q.wait()
        if n == 7:
            for h in range(2):
                landed(r1d.at[h, 0], p1d.at[h, 0])
                first = rows(line(h, 1), half)
                s1[first, :] = (keep[h, 0] + r1d[h, 0].astype(F32)).astype(BF16)
                go("first", s1.at[first], r1p.at[h, 0], p1r.at[h], up(h))
                landed(r1d.at[h, 1], p1d.at[h, 1])
                second = rows(line(h, 3) + half, half)
                s1[second, :] = (keep[h, 1] + r1d[h, 1].astype(F32)).astype(BF16)
                go("first", s1.at[second], r1p.at[h, 1], p1r.at[h], down(h))
        for h in range(2):
            if whose:
                take(i, h)
            else:
                give(i, h)

    load_momentum = pltpu.make_async_copy(momentum, held, ld.at[9])
    load_momentum.start()

    for h in range(2):
        landed(span(s1, 2 * LINE), p1r.at[h])
        o1[h, :half] += r1p[h, 0].astype(F32) + r1o[h, 1].astype(F32)
        o1[h, half:] += r1o[h, 0].astype(F32) + r1p[h, 1].astype(F32)
        if h == 0:
            sx[0] = o1[0].astype(BF16)
            o1[0] = jnp.dot(sx[0], q[...], preferred_element_type=F32)
        s2[h] = o1[h].astype(BF16)
        for i in (2, 1, 3):
            b = turn(c2[h], i, NY)
            go("second", s2.at[h, rows(b * SUB, SUB)], r2.at[h, c2[h]], p2r.at[h], peer2(h, b))
    for h in range(2):
        landed(r2.at[h, pl.ds(0, NY - 1)], p2r.at[h])
        total = o1[h, rows(c2[h] * SUB, SUB), :]
        for i in range(1, NY):
            total += r2[h, turn(c2[h], i, NY)].astype(F32)
        for c in range(2):
            o3[h, c] = total[:, c * HALF:(c + 1) * HALF]
            s3[h, c] = total[:, c * HALF:(c + 1) * HALF].astype(BF16)

    far = (4, 3, 5, 2, 6, 1, 7)

    def spot(v):
        return v // 4, rows((v % 4) * TILE, TILE)

    for i in far:
        b = turn(z, i, NZ)
        c, at = spot(b)
        go("z", s3.at[:, c, at], r3.at[z], oner.at[0], device(x, y, b, core))
    for i in (2, 1, 3):
        b = turn(x, i, NX)
        go("merged", xs.at[:, b], rx.at[x], oner.at[1], device(b, y, z, core))
    sent("core", span(left, 2 * PART))
    sent("first", span(left, 6 * LINE))
    sent("second", span(left, 6 * SUB))
    landed(span(r3, NZ - 1), oner.at[0])

    def sub(h, i, j):
        return rows(mine + line(h, i) + turn(c2[h], j, NY) * SUB, SUB)

    c, at = spot(z)
    for h in range(2):
        total = o3[h, c, at, :]
        for i in range(1, NZ):
            total += r3[turn(z, i, NZ), h].astype(F32)
        g3[z, h] = total.astype(BF16)
    for i in far:
        b = turn(z, i, NZ)
        go("tiles", g3.at[z], g3.at[z], oner.at[2], device(x, y, b, core))

    def along(h, j):
        at, b = left.at[sub(h, 0, j)], turn(c2[h], j, NY)
        go("lines", at, at, a1r.at[h, 0, b], up(h))
        go("lines", at, at, a1r.at[h, 1, b], down(h))

    def arrive(h, side, j):
        at, b = left.at[sub(h, 3 if side == 0 else 1, j)], turn(c2[h], j, NY)
        landed(at, a1r.at[h, side, b])

    def relay(h, side, j):
        at, b = left.at[sub(h, 3 if side == 0 else 1, j)], turn(c2[h], j, NY)
        go("lines", at, at, axr.at[h, b], up(h) if side == 0 else down(h))

    def cross(h, i):
        at = left.at[rows(mine + line(h, i), LINE)]
        go("cross", at, at, oner.at[3], sibling)

    def across_rows(a, b):
        return lax.dot_general(a, b, (((0,), (0,)), ((), ())), preferred_element_type=F32)

    def products(h, i):
        part = left[rows(mine + line(h, i), LINE), :]
        gpart[h * NX + turn(c1[h], i, NX)] = across_rows(part, part)

    def far_line(h, j):
        at, b = left.at[sub(h, 2, j)], turn(c2[h], j, NY)
        landed(at, axr.at[h, b])

    landed(span(g3, NZ - 1), oner.at[2])
    for h in range(2):
        left[sub(h, 0, 0), :] = jnp.concatenate(
            [jnp.concatenate([g3[c * 4 + v, h] for c in range(2)], axis=1) for v in range(4)], axis=0
        )
        at = left.at[sub(h, 0, 0)]
        for i in (2, 1, 3):
            b = turn(c2[h], i, NY)
            go("gather", at, at, a2r.at[h, c2[h]], peer2(h, b))
        along(h, 0)
    for j in (1, 3, 2):
        for h in range(2):
            at, b = left.at[sub(h, 0, j)], turn(c2[h], j, NY)
            landed(at, a2r.at[h, b])
            along(h, j)
    for j, side in ((0, 0), (1, 0), (3, 1), (2, 1)):
        for h in range(2):
            arrive(h, side, j)
            relay(h, side, j)
    for h in range(2):
        cross(h, 0)

    owner = x * 2 + core
    others = [(turn(x, i, NX), lax.rem(core + e, 2)) for i in range(NX) for e in range(2) if i or e]

    def piece(v, c):
        return rows((v * 2 + c) * PIECE, PIECE)

    total = across_rows(left[rows(mine + line(0, 0), LINE), :], sx[0])
    landed(span(rx, NX - 1), oner.at[1])
    owned = xs[:, x].astype(F32)
    for i in range(1, NX):
        owned += rx[turn(x, i, NX)].astype(F32)
    sx[1] = owned.astype(BF16).reshape(LINE, RANK)
    arrive(1, 1, 0)
    far_line(1, 0)
    owned = jnp.concatenate([left[rows(mine + PART + v * LINE + x * SUB, SUB), :] for v in range(NY)], axis=0)
    zsum[...] = total + across_rows(owned, sx[1])
    zsend[...] = zsum[...].astype(BF16)
    for v, c in others:
        go("right", zsend.at[piece(v, c)], zr.at[owner], oner.at[5], device(v, y, z, c))

    for h in range(2):
        products(h, 0)
    for h in range(2):
        arrive(h, 0, 3)
        arrive(h, 0, 2)
        cross(h, 3)
        products(h, 3)
    for h in range(2):
        if h == 0:
            arrive(h, 1, 0)
        arrive(h, 1, 1)
        cross(h, 1)
        products(h, 1)
    for h in range(2):
        for j in (0, 1, 3, 2)[h:]:
            far_line(h, j)
        products(h, 2)

    total = gpart[0]
    for i in range(1, 2 * NX):
        total += gpart[i]
    gsum[...] = total
    go("gram", gsum, gin, oner.at[4], sibling)

    for h in range(2):
        cross(h, 2)
    across = device(x, y, turn(z, ZLO, NZ), core)

    def add_pieces():
        landed(span(zr, OWNERS - 1), oner.at[5])
        total = zsum[piece(x, core), :]
        for v, c in others:
            total += zr[v * 2 + c].astype(F32)
        zown[...] = total.astype(BF16)
        go("across", zown, zpair, oner.at[6], across)

    def add_across():
        landed(zpair, oner.at[6])
        here = piece(x, core)
        zall[here, :] = (zown[...].astype(F32) + zpair[...].astype(F32)).astype(BF16)
        for v, c in others:
            go("back", zall.at[here], zall.at[here], oner.at[7], device(v, y, z, c))

    add_pieces()
    sent("z", span(r3, NZ - 1))
    sent("merged", span(rx, NX - 1))
    sent("tiles", span(r3, NZ - 1))
    sent("gather", span(left, 6 * SUB))
    sent("lines", span(left, 24 * SUB))
    landed(gin, oner.at[4])
    inverse = inverse_factor(gsum[...] + gin[...], ({}, {3: add_across}))
    landed(span(zall, (OWNERS - 1) * PIECE), oner.at[7])
    w1 = inverse.astype(BF16)
    w2 = (inverse - w1.astype(F32)).astype(BF16)

    def apply(matrix, dim):
        dims = (((dim,), (0,)), ((), ()))
        return sum(lax.dot_general(w, matrix, dims, preferred_element_type=F32) for w in (w1, w2))

    factor = (apply(zall[...], 1) / PODS).astype(BF16)
    new_factor[...] = factor.T
    mix = apply(factor, 0)
    head = mix.astype(BF16)
    high[...] = head
    low[...] = (mix - head.astype(F32)).astype(BF16)

    landed(span(left, MINE), oner.at[3])
    load_momentum.wait()
    sent("cross", span(left, MINE))
    sent("gram", gsum)
    sent("right", span(zr, OWNERS - 1))
    sent("across", zown)
    sent("back", span(zr, OWNERS - 1))


def gather(delta, error, momentum, q):
    vmem, hbm = (pl.BlockSpec(memory_space=s) for s in (pltpu.VMEM, pltpu.HBM))
    dma = pltpu.SemaphoreType.DMA
    wide, square = (ROWS, RANK), (RANK, RANK)
    return pl.pallas_call(
        exchange,
        out_shape=(
            jax.ShapeDtypeStruct(wide, BF16),
            jax.ShapeDtypeStruct(wide, BF16),
            jax.ShapeDtypeStruct(wide, BF16),
            jax.ShapeDtypeStruct(square, BF16),
            jax.ShapeDtypeStruct(square, BF16),
            jax.ShapeDtypeStruct(square, BF16),
        ),
        in_specs=[hbm] * 4,
        out_specs=(vmem,) * 6,
        scratch_shapes=[
            pltpu.VMEM(square, BF16),
            pltpu.VMEM(wide, BF16),
            pltpu.VMEM(wide, BF16),
            pltpu.VMEM((MINE, RANK), BF16),
            pltpu.VMEM((MINE, RANK), BF16),
            pltpu.VMEM((NY, NX, SUB, RANK), BF16),
            pltpu.VMEM((NX, NY, SUB, RANK), BF16),
            pltpu.VMEM((2, LINE, RANK), BF16),
            pltpu.VMEM((2, 2, LINE // 2, RANK), F32),
            pltpu.VMEM((2, 2, LINE // 2, RANK), BF16),
            pltpu.VMEM((2, 2, LINE // 2, RANK), BF16),
            pltpu.VMEM((2, 2, LINE // 2, RANK), BF16),
            pltpu.VMEM((2, LINE, RANK), F32),
            pltpu.VMEM((2, LINE, RANK), BF16),
            pltpu.VMEM((2, NY, SUB, RANK), BF16),
            pltpu.VMEM((2, 2, SUB, HALF), BF16),
            pltpu.VMEM((NZ, 2, TILE, HALF), BF16),
            pltpu.VMEM((2, 2, SUB, HALF), F32),
            pltpu.VMEM((NZ, 2, TILE, HALF), BF16),
            pltpu.VMEM((2 * NX,) + square, F32),
            pltpu.VMEM(square, F32),
            pltpu.VMEM(square, F32),
            pltpu.VMEM(square, F32),
            pltpu.VMEM(square, BF16),
            pltpu.VMEM((OWNERS, PIECE, RANK), BF16),
            pltpu.VMEM((PIECE, RANK), BF16),
            pltpu.VMEM((PIECE, RANK), BF16),
            pltpu.VMEM(square, BF16),
            dma((10,)), dma((13,)), dma((NX,)), dma((2, 2)), dma((2,)), dma((2,)), dma((8,)),
            dma((2, NY)), dma((2, 2, NY)), dma((2, NY)),
        ],
        compiler_params=pltpu.CompilerParams(collective_id=0, has_side_effects=True, vmem_limit_bytes=32 << 20),
        cost_estimate=pl.CostEstimate(flops=6 * ROWS * RANK * RANK, bytes_accessed=5 * ROWS * RANK * 2, transcendentals=0),
        name="gather_left",
    )(*(pltpu.with_memory_space_constraint(a, pltpu.HBM) for a in (delta, error, momentum, q)))


def finish(left, merged, momentum, high, low, factor, new_error, new_momentum, outer_step, new_factor, e, m, s, sem):
    size, count = ROWS // 8, 8
    copies = [pltpu.make_async_copy(factor, new_factor, sem.at[count, 0])]
    copies[0].start()
    for i in range(count):
        at = pl.ds(i * size, size)
        block = left[at, :]
        approx = jnp.dot(block, high[...], preferred_element_type=F32) + jnp.dot(
            block, low[...], preferred_element_type=F32
        )
        e[at, :] = (merged[at, :].astype(F32) - approx).astype(BF16)
        moment = 0.9 * momentum[at, :].astype(F32) + approx
        m[at, :] = moment.astype(BF16)
        s[at, :] = (0.7 * (approx + 0.9 * moment)).astype(BF16)
        for k, (src, dst) in enumerate(((e, new_error.at[0, at]), (m, new_momentum.at[at]), (s, outer_step.at[at]))):
            copies.append(pltpu.make_async_copy(src.at[at], dst, sem.at[i, k]))
            copies[-1].start()
    for copy in copies:
        copy.wait()


def outputs(left, merged, momentum, high, low, factor):
    any_, vmem = pl.BlockSpec(memory_space=pl.ANY), pl.BlockSpec(memory_space=pltpu.VMEM)
    wide = (ROWS, RANK)
    return pl.pallas_call(
        finish,
        out_shape=(
            jax.ShapeDtypeStruct((1,) + wide, BF16),
            jax.ShapeDtypeStruct(wide, BF16),
            jax.ShapeDtypeStruct(wide, BF16),
            jax.ShapeDtypeStruct((RANK, RANK), BF16),
        ),
        in_specs=[vmem] * 6,
        out_specs=(any_,) * 4,
        scratch_shapes=[pltpu.VMEM(wide, BF16)] * 3 + [pltpu.SemaphoreType.DMA((9, 3))],
        compiler_params=pltpu.CompilerParams(vmem_limit_bytes=24 << 20),
        cost_estimate=pl.CostEstimate(flops=4 * ROWS * RANK * RANK, bytes_accessed=6 * ROWS * RANK * 2, transcendentals=0),
        name="outputs",
    )(left, merged, momentum, high, low, factor)


def body(delta, error, momentum, q_init):
    left, merged, held, high, low, factor = gather(delta, error, momentum, q_init)
    return outputs(left, merged, held, high, low, factor)


def solution(mesh):
    placed = (P("outer", None, "tp"), P("outer", None, "tp"), P(None, "tp"), P("tp", None))
    return jax.shard_map(
        body,
        mesh=mesh,
        in_specs=placed,
        out_specs=(P("outer", None, "tp"), P(None, "tp"), P(None, "tp"), P("tp", None)),
        check_vma=False,
    )
```

time: 68.8 us -> 67.6 us (0.983)
  Pallas kernels: 68.1 us -> 66.8 us
    pallas_call x1, Pallas kernels: 64.6 us -> 63.4 us  [gather(): pl.pallas_call(exchange, out_shape=(jax.ShapeDtypeStruct(wide, BF16), jax...]
where the time goes in v2:
time: 67.6 us; the launch traced here: 67.5 us
  Pallas kernels  66.8 us (99%)
    pallas_call x1, Pallas kernels, gather(): pl.pallas_call(exchange, out_shape=(jax.ShapeDtypeStruct(wide, BF16), jax...  63.4 us
    pallas_call x1, Pallas kernels, outputs(): pl.pallas_call(finish, out_shape=(jax.ShapeDtypeStruct((1,) + wide, BF16)...  3.47 us

profile of v2, /device:TPU:1, one launch (start us, length us, event | category | flops | bytes accessed | tf_op | source)
XLA Modules:
  0.0 67.5 jit_solution(17558725336003754101)
XLA Ops:
  0.6 63.4 %gather_left.1 = (bf16[4096,256]{1,0:T(8,128)(2,1)S(1)}, bf16[4096,256]{1,0:T(8,128)(2,1)S(1)}, bf16[4096,256]{1,0:T(8,128)(2,1)S(1)}, bf16[256,256]{1,0:T(8,128...) custom-call(bf16[1,4096,256]{2,1,0:T(8,128)(2,1)} %delta.1, bf16[1,4096,256]{2,1,0:T(8,128)(2,1)} %error.1, ...), custom_call_target="tpu_custom_call" | custom-call | flops 1610612736 | bytes 10485760 | tf_op jit(solution)/shard_map/gather_left/pallas_call | solution.py:455
  64.0 3.5 %outputs.1 = (bf16[1,4096,256]{2,1,0:T(8,128)(2,1)}, bf16[4096,256]{1,0:T(8,128)(2,1)}, bf16[4096,256]{1,0:T(8,128)(2,1)}, bf16[256,256]{1,0:T(8,128)(2,1)}) custom-call(bf16[4096,256]{1,0:T(8,128)(2,1)S(1)} %get-tuple-element.10.left, bf16[4096,256]{1,0:T(8,128)(2,1)S(1)} %get-tuple-element.11.merged, bf16[4096,256]{1,0:T(8,128)(2,1)S(1)} %get-tuple-element.12.momentum, ...), custom_call_target="tpu_custom_call" | custom-call | flops 1073741824 | bytes 12582912 | tf_op jit(solution)/shard_map/outputs/pallas_call | solution.py:529

commit v3 on v2

--- a/solution.py
+++ b/solution.py
@@ -113,9 +113,9 @@
 
 def exchange(
     delta, error, momentum, q_in, left, merged, held, high, low, new_factor,
-    q, dbuf, ebuf, pair_in, s1, xs, rx, sx, keep, r1o, r1d, r1p, o1, s2, r2, s3, r3, o3, g3,
+    q, dbuf, ebuf, pair_in, s1, xs, rx, sx, r1, o1, s2, r2, s3, r3, o3, g3,
     gpart, gsum, gin, zsum, zsend, zr, zown, zpair, zall,
-    ld, ss, cr, p1d, p1r, p2r, oner, a2r, a1r, axr,
+    ld, ss, cr, p1r, p2r, oner, a2r, a1r,
 ):
     o, t = lax.axis_index("outer"), lax.axis_index("tp")
     core, x, y = lax.rem(o, 2), lax.rem(o // 2, NX), lax.rem(t, NY)
@@ -188,14 +188,6 @@
         total = (dbuf[block, :].astype(F32) + ebuf[block, :].astype(F32)).astype(BF16)
         merged[block, :] = total
         return block, total.astype(F32)
-
-    half = LINE // 2
-
-    def up(h):
-        return peer1(h, turn(c1[h], 1, NX))
-
-    def down(h):
-        return peer1(h, turn(c1[h], NX - 1, NX))
 
     def give(i, h):
         block, _ = merge(0, i, h)
@@ -213,19 +205,9 @@
             both = total.astype(BF16)
             xs[turn(y, i, NY)] = both.reshape(NX, SUB, RANK)
             total = jnp.dot(both, q[...], preferred_element_type=F32)
-        first, second = rows(at, half), rows(at + half, half)
-        if i == 2:
+        if i:
             s1[here, :] = total.astype(BF16)
-            go("first", s1.at[first], r1d.at[h, 0], p1d.at[h, 0], up(h))
-            go("first", s1.at[second], r1d.at[h, 1], p1d.at[h, 1], down(h))
-        elif i == 1:
-            s1[second, :] = total[half:].astype(BF16)
-            go("first", s1.at[second], r1o.at[h, 0], p1r.at[h], up(h))
-            keep[h, 0] = total[:half]
-        elif i == 3:
-            s1[first, :] = total[:half].astype(BF16)
-            go("first", s1.at[first], r1o.at[h, 1], p1r.at[h], down(h))
-            keep[h, 1] = total[half:]
+            go("first", s1.at[here], r1.at[h, c1[h]], p1r.at[h], peer1(h, turn(c1[h], i, NX)))
         else:
             o1[h] = total
 
@@ -234,16 +216,6 @@
             pl.semaphore_wait(barrier, len(greeted))
         if n == 2:
             load_q.wait()
-        if n == 7:
-            for h in range(2):
-                landed(r1d.at[h, 0], p1d.at[h, 0])
-                first = rows(line(h, 1), half)
-                s1[first, :] = (keep[h, 0] + r1d[h, 0].astype(F32)).astype(BF16)
-                go("first", s1.at[first], r1p.at[h, 0], p1r.at[h], up(h))
-                landed(r1d.at[h, 1], p1d.at[h, 1])
-                second = rows(line(h, 3) + half, half)
-                s1[second, :] = (keep[h, 1] + r1d[h, 1].astype(F32)).astype(BF16)
-                go("first", s1.at[second], r1p.at[h, 1], p1r.at[h], down(h))
         for h in range(2):
             if whose:
                 take(i, h)
@@ -254,9 +226,11 @@
     load_momentum.start()
 
     for h in range(2):
-        landed(span(s1, 2 * LINE), p1r.at[h])
-        o1[h, :half] += r1p[h, 0].astype(F32) + r1o[h, 1].astype(F32)
-        o1[h, half:] += r1o[h, 0].astype(F32) + r1p[h, 1].astype(F32)
+        landed(span(s1, 3 * LINE), p1r.at[h])
+        total = o1[h]
+        for i in range(1, NX):
+            total += r1[h, turn(c1[h], i, NX)].astype(F32)
+        o1[h] = total
         if h == 0:
             sx[0] = o1[0].astype(BF16)
             o1[0] = jnp.dot(sx[0], q[...], preferred_element_type=F32)
@@ -305,16 +279,11 @@
 
     def along(h, j):
         at, b = left.at[sub(h, 0, j)], turn(c2[h], j, NY)
-        go("lines", at, at, a1r.at[h, 0, b], up(h))
-        go("lines", at, at, a1r.at[h, 1, b], down(h))
-
-    def arrive(h, side, j):
-        at, b = left.at[sub(h, 3 if side == 0 else 1, j)], turn(c2[h], j, NY)
-        landed(at, a1r.at[h, side, b])
-
-    def relay(h, side, j):
-        at, b = left.at[sub(h, 3 if side == 0 else 1, j)], turn(c2[h], j, NY)
-        go("lines", at, at, axr.at[h, b], up(h) if side == 0 else down(h))
+        for i in (2, 1, 3):
+            go("lines", at, at, a1r.at[h, c1[h], b], peer1(h, turn(c1[h], i, NX)))
+
+    def arrive(h, i, j):
+        landed(left.at[sub(h, i, j)], a1r.at[h, turn(c1[h], i, NX), turn(c2[h], j, NY)])
 
     def cross(h, i):
         at = left.at[rows(mine + line(h, i), LINE)]
@@ -326,10 +295,6 @@
     def products(h, i):
         part = left[rows(mine + line(h, i), LINE), :]
         gpart[h * NX + turn(c1[h], i, NX)] = across_rows(part, part)
-
-    def far_line(h, j):
-        at, b = left.at[sub(h, 2, j)], turn(c2[h], j, NY)
-        landed(at, axr.at[h, b])
 
     landed(span(g3, NZ - 1), oner.at[2])
     for h in range(2):
@@ -346,10 +311,6 @@
             at, b = left.at[sub(h, 0, j)], turn(c2[h], j, NY)
             landed(at, a2r.at[h, b])
             along(h, j)
-    for j, side in ((0, 0), (1, 0), (3, 1), (2, 1)):
-        for h in range(2):
-            arrive(h, side, j)
-            relay(h, side, j)
     for h in range(2):
         cross(h, 0)
 
@@ -365,8 +326,8 @@
     for i in range(1, NX):
         owned += rx[turn(x, i, NX)].astype(F32)
     sx[1] = owned.astype(BF16).reshape(LINE, RANK)
-    arrive(1, 1, 0)
-    far_line(1, 0)
+    for i in (1, 3, 2):
+        arrive(1, i, 0)
     owned = jnp.concatenate([left[rows(mine + PART + v * LINE + x * SUB, SUB), :] for v in range(NY)], axis=0)
     zsum[...] = total + across_rows(owned, sx[1])
     zsend[...] = zsum[...].astype(BF16)
@@ -375,21 +336,13 @@
 
     for h in range(2):
         products(h, 0)
-    for h in range(2):
-        arrive(h, 0, 3)
-        arrive(h, 0, 2)
-        cross(h, 3)
-        products(h, 3)
-    for h in range(2):
-        if h == 0:
-            arrive(h, 1, 0)
-        arrive(h, 1, 1)
-        cross(h, 1)
-        products(h, 1)
-    for h in range(2):
-        for j in (0, 1, 3, 2)[h:]:
-            far_line(h, j)
-        products(h, 2)
+    for i in (1, 3, 2):
+        for h in range(2):
+            for j in (0, 1, 3, 2)[h:]:
+                arrive(h, i, j)
+            if i != 2:
+                cross(h, i)
+            products(h, i)
 
     total = gpart[0]
     for i in range(1, 2 * NX):
@@ -473,10 +426,7 @@
             pltpu.VMEM((NY, NX, SUB, RANK), BF16),
             pltpu.VMEM((NX, NY, SUB, RANK), BF16),
             pltpu.VMEM((2, LINE, RANK), BF16),
-            pltpu.VMEM((2, 2, LINE // 2, RANK), F32),
-            pltpu.VMEM((2, 2, LINE // 2, RANK), BF16),
-            pltpu.VMEM((2, 2, LINE // 2, RANK), BF16),
-            pltpu.VMEM((2, 2, LINE // 2, RANK), BF16),
+            pltpu.VMEM((2, NX, LINE, RANK), BF16),
             pltpu.VMEM((2, LINE, RANK), F32),
             pltpu.VMEM((2, LINE, RANK), BF16),
             pltpu.VMEM((2, NY, SUB, RANK), BF16),
@@ -493,8 +443,7 @@
             pltpu.VMEM((PIECE, RANK), BF16),
             pltpu.VMEM((PIECE, RANK), BF16),
             pltpu.VMEM(square, BF16),
-            dma((10,)), dma((13,)), dma((NX,)), dma((2, 2)), dma((2,)), dma((2,)), dma((8,)),
-            dma((2, NY)), dma((2, 2, NY)), dma((2, NY)),
+            dma((10,)), dma((13,)), dma((NX,)), dma((2,)), dma((2,)), dma((8,)), dma((2, NY)), dma((2, NX, NY)),
         ],
         compiler_params=pltpu.CompilerParams(collective_id=0, has_side_effects=True, vmem_limit_bytes=32 << 20),
         cost_estimate=pl.CostEstimate(flops=6 * ROWS * RANK * RANK, bytes_accessed=5 * ROWS * RANK * 2, transcendentals=0),

time: 67.6 us -> 66.9 us (0.990)
  no operation moved by 1% of the time
where the time goes in v3:
time: 66.9 us; the launch traced here: 66.8 us
  Pallas kernels  66.2 us (99%)
    pallas_call x1, Pallas kernels, gather(): pl.pallas_call(exchange, out_shape=(jax.ShapeDtypeStruct(wide, BF16), jax...  62.7 us
    pallas_call x1, Pallas kernels, outputs(): pl.pallas_call(finish, out_shape=(jax.ShapeDtypeStruct((1,) + wide, BF16)...  3.47 us

profile of v3, /device:TPU:1, one launch (start us, length us, event | category | flops | bytes accessed | tf_op | source)
XLA Modules:
  0.0 66.8 jit_solution(11832030843645002684)
XLA Ops:
  0.6 62.7 %gather_left.1 = (bf16[4096,256]{1,0:T(8,128)(2,1)S(1)}, bf16[4096,256]{1,0:T(8,128)(2,1)S(1)}, bf16[4096,256]{1,0:T(8,128)(2,1)S(1)}, bf16[256,256]{1,0:T(8,128...) custom-call(bf16[1,4096,256]{2,1,0:T(8,128)(2,1)} %delta.1, bf16[1,4096,256]{2,1,0:T(8,128)(2,1)} %error.1, ...), custom_call_target="tpu_custom_call" | custom-call | flops 1610612736 | bytes 10485760 | tf_op jit(solution)/shard_map/gather_left/pallas_call | solution.py:408
  63.4 3.5 %outputs.1 = (bf16[1,4096,256]{2,1,0:T(8,128)(2,1)}, bf16[4096,256]{1,0:T(8,128)(2,1)}, bf16[4096,256]{1,0:T(8,128)(2,1)}, bf16[256,256]{1,0:T(8,128)(2,1)}) custom-call(bf16[4096,256]{1,0:T(8,128)(2,1)S(1)} %get-tuple-element.10.left, bf16[4096,256]{1,0:T(8,128)(2,1)S(1)} %get-tuple-element.11.merged, bf16[4096,256]{1,0:T(8,128)(2,1)S(1)} %get-tuple-element.12.momentum, ...), custom_call_target="tpu_custom_call" | custom-call | flops 1073741824 | bytes 12582912 | tf_op jit(solution)/shard_map/outputs/pallas_call | solution.py:478

commit v4 on v3

--- a/solution.py
+++ b/solution.py
@@ -35,54 +35,65 @@
     lane = lax.broadcasted_iota(jnp.int32, tile, 1)
     row = lax.broadcasted_iota(jnp.int32, tile, 0)
     tiles = a.reshape(16, 8, 128)
-    both, rest = tiles[:2], tiles[2:]
+    pivots, following, rest = tiles[0], tiles[1], tiles[2:]
     done = []
     for g in range(16):
         first = 8 * g
-        shape = both.shape
-        below = shape[0] - 1
-        cols = [jnp.broadcast_to(both[:, :, first + c:first + c + 1], shape) for c in range(8)]
         here = (lane >= first) & (lane < first + 8)
-        start = [jnp.where(here, jnp.where(lane - first == row, 1.0, 0.0), both[0])]
-        start += [jnp.where(here, 0.0, both[1])] * below
-        both = jnp.stack(start)
+
+        def column(x, c):
+            return jnp.broadcast_to(x[:, first + c:first + c + 1], tile)
+
+        def line(x, r):
+            return jnp.broadcast_to(x[r:r + 1], tile)
+
+        lefts = [column(pivots, c) for c in range(8)]
+        block = {(r, c): line(lefts[c], r) for c in range(8) for r in range(c, 8)}
+        own = jnp.where(here, jnp.where(lane - first == row, 1.0, 0.0), pivots)
+        lines = [line(own, r) for r in range(8)]
+        if g < 15:
+            below = [column(following, c) for c in range(8)]
+            following = jnp.where(here, 0.0, following)
         diag = jnp.ones(tile, F32)
-
-        def spread(x, r):
-            return jnp.broadcast_to(x[0, r:r + 1], tile)
-
-        def after(r, x):
-            top = jnp.where(row > r, x[:1], 0.0)
-            return jnp.concatenate([top, x[1:]], axis=0) if below else top
-
+        upper = own
+        inverses = []
         for p in range(0, 8, 2):
             q = p + 1
-            d_p, d_pq, d_q = spread(cols[p], p), spread(cols[p], q), spread(cols[q], q)
+            d_p, d_pq, d_q = block[p, p], block[q, p], block[q, q]
             det = d_p * d_q - d_pq * d_pq
             inv_p = reciprocal(d_p)
             inv_q = d_p * reciprocal(det)
             ratio = d_pq * inv_p
-            line_p = spread(both, p)
-            line_q = spread(both, q) - ratio * line_p
+            inverses += [inv_p, inv_q]
+            lines[q] = lines[q] - ratio * lines[p]
             diag = jnp.where(row == p, d_p, jnp.where(row == q, det * inv_p, diag))
-            part_p = after(p, cols[p] * inv_p)
-            part_q = after(q, (cols[q] - part_p * d_pq) * inv_q)
-            both = both - part_p * line_p - part_q * line_q
-            for k in range(q + 1, 8):
-                edge_p = spread(cols[k], p)
-                edge_q = spread(cols[k], q) - ratio * edge_p
-                cols[k] = cols[k] - part_p * edge_p - part_q * edge_q
-        upper = both[0]
+            upper = jnp.where(row == q, lines[q], upper)
+            later = range(q + 1, 8)
+            edge_p = {k: block[k, p] for k in later}
+            edge_q = {k: block[k, q] - ratio * edge_p[k] for k in later}
+            part_p = {k: edge_p[k] * inv_p for k in later}
+            part_q = {k: edge_q[k] * inv_q for k in later}
+            for c in later:
+                for r in range(c, 8):
+                    block[r, c] = block[r, c] - part_p[r] * edge_p[c] - part_q[r] * edge_q[c]
+            for k in later:
+                lines[k] = lines[k] - part_p[k] * lines[p] - part_q[k] * lines[q]
+                upper = jnp.where(row == k, lines[k], upper) if k == q + 1 else upper
+            if g < 15:
+                below_p = below[p] * inv_p
+                below_q = (below[q] - below_p * d_pq) * inv_q
+                following = following - below_p * lines[p] - below_q * lines[q]
+                for k in later:
+                    below[k] = below[k] - below_p * edge_p[k] - below_q * edge_q[k]
         done.append(jnp.where(lane <= row + first, upper * (1.0 / jnp.sqrt(diag)), 0.0))
         if g < 14:
             factors = (upper / diag).T[first + 16:].reshape(rest.shape[0], 8, 8)
             rest = jnp.where(here, 0.0, rest)
             for c in range(8):
-                rest = rest - factors[:, :, c:c + 1] * upper[c:c + 1]
-            both = jnp.concatenate([both[1:], rest[:1]], axis=0)
-            rest = rest[1:] if g < 13 else None
-        elif g < 15:
-            both = both[1:]
+                rest = rest - factors[:, :, c:c + 1] * lines[c]
+            pivots, following, rest = following, rest[0], rest[1:] if g < 13 else None
+        elif g == 14:
+            pivots = following
         if g in between:
             between[g]()
     return jnp.concatenate(done, axis=0)
@@ -95,8 +106,9 @@
     gram = gram * scale * (1.0 / jnp.sqrt(jnp.sum(diagonal, axis=1, keepdims=True)))
     w11 = factor_block(gram[:128, :128], between[0])
     l21 = mm(gram[128:, :128], w11, ((1,), (1,)))
+    corner = mm(l21, w11, ((1,), (0,)))
     w22 = factor_block(gram[128:, 128:] - mm(l21, l21, ((1,), (1,))), between[1])
-    w21 = -mm(w22, mm(l21, w11, ((1,), (0,))), ((1,), (0,)))
+    w21 = -mm(w22, corner, ((1,), (0,)))
     top = jnp.concatenate([w11, jnp.zeros((128, 128), F32)], axis=1)
     return jnp.concatenate([top, jnp.concatenate([w21, w22], axis=1)], axis=0) * scale
 
@@ -112,8 +124,8 @@
 
 
 def exchange(
-    delta, error, momentum, q_in, left, merged, held, high, low, new_factor,
-    q, dbuf, ebuf, pair_in, s1, xs, rx, sx, r1, o1, s2, r2, s3, r3, o3, g3,
+    delta, error, momentum, q_in, left, merged, held, mixed, new_factor,
+    q, dbuf, ebuf, pair_in, s1, xs, rx, sx, r1, o1, o2, s2, r2, s3, r3, o3, g3,
     gpart, gsum, gin, zsum, zsend, zr, zown, zpair, zall,
     ld, ss, cr, p1r, p2r, oner, a2r, a1r,
 ):
@@ -149,6 +161,13 @@
             pltpu.make_async_copy(error.at[0, src], ebuf.at[src], ld.at[k]),
         )
 
+    def fetch(part):
+        for whose, i in part:
+            for h in range(2):
+                for copy in loads(whose, i, h):
+                    copy.start()
+
+    fetch(order[:2])
     barrier = pltpu.get_barrier_semaphore()
     greeted = [sibling]
     greeted += [device(turn(x, i, NX), y, z, core) for i in range(1, NX)]
@@ -158,10 +177,7 @@
     for dev in greeted:
         pl.semaphore_signal(barrier, inc=1, device_id=dev, device_id_type=MESH)
 
-    for whose, i in order:
-        for h in range(2):
-            for copy in loads(whose, i, h):
-                copy.start()
+    fetch(order[2:])
     load_q = pltpu.make_async_copy(q_in, q, ld.at[8])
     load_q.start()
 
@@ -227,20 +243,24 @@
 
     for h in range(2):
         landed(span(s1, 3 * LINE), p1r.at[h])
-        total = o1[h]
-        for i in range(1, NX):
-            total += r1[h, turn(c1[h], i, NX)].astype(F32)
-        o1[h] = total
-        if h == 0:
-            sx[0] = o1[0].astype(BF16)
-            o1[0] = jnp.dot(sx[0], q[...], preferred_element_type=F32)
-        s2[h] = o1[h].astype(BF16)
-        for i in (2, 1, 3):
+        for i in (2, 1, 3, 0):
             b = turn(c2[h], i, NY)
-            go("second", s2.at[h, rows(b * SUB, SUB)], r2.at[h, c2[h]], p2r.at[h], peer2(h, b))
+            at = rows(b * SUB, SUB)
+            total = o1[h, at, :]
+            for j in range(1, NX):
+                total += r1[h, turn(c1[h], j, NX), at, :].astype(F32)
+            if h == 0:
+                both = total.astype(BF16)
+                sx[0, at, :] = both
+                total = jnp.dot(both, q[...], preferred_element_type=F32)
+            if i:
+                s2[h, at, :] = total.astype(BF16)
+                go("second", s2.at[h, at], r2.at[h, c2[h]], p2r.at[h], peer2(h, b))
+            else:
+                o2[h] = total
     for h in range(2):
         landed(r2.at[h, pl.ds(0, NY - 1)], p2r.at[h])
-        total = o1[h, rows(c2[h] * SUB, SUB), :]
+        total = o2[h]
         for i in range(1, NY):
             total += r2[h, turn(c2[h], i, NY)].astype(F32)
         for c in range(2):
@@ -306,6 +326,11 @@
             b = turn(c2[h], i, NY)
             go("gather", at, at, a2r.at[h, c2[h]], peer2(h, b))
         along(h, 0)
+    landed(span(rx, NX - 1), oner.at[1])
+    owned = xs[:, x].astype(F32)
+    for i in range(1, NX):
+        owned += rx[turn(x, i, NX)].astype(F32)
+    sx[1] = owned.astype(BF16).reshape(LINE, RANK)
     for j in (1, 3, 2):
         for h in range(2):
             at, b = left.at[sub(h, 0, j)], turn(c2[h], j, NY)
@@ -321,11 +346,6 @@
         return rows((v * 2 + c) * PIECE, PIECE)
 
     total = across_rows(left[rows(mine + line(0, 0), LINE), :], sx[0])
-    landed(span(rx, NX - 1), oner.at[1])
-    owned = xs[:, x].astype(F32)
-    for i in range(1, NX):
-        owned += rx[turn(x, i, NX)].astype(F32)
-    sx[1] = owned.astype(BF16).reshape(LINE, RANK)
     for i in (1, 3, 2):
         arrive(1, i, 0)
     owned = jnp.concatenate([left[rows(mine + PART + v * LINE + x * SUB, SUB), :] for v in range(NY)], axis=0)
@@ -389,8 +409,8 @@
     new_factor[...] = factor.T
     mix = apply(factor, 0)
     head = mix.astype(BF16)
-    high[...] = head
-    low[...] = (mix - head.astype(F32)).astype(BF16)
+    mixed[:RANK, :] = head
+    mixed[RANK:, :] = (mix - head.astype(F32)).astype(BF16)
 
     landed(span(left, MINE), oner.at[3])
     load_momentum.wait()
@@ -411,12 +431,11 @@
             jax.ShapeDtypeStruct(wide, BF16),
             jax.ShapeDtypeStruct(wide, BF16),
             jax.ShapeDtypeStruct(wide, BF16),
-            jax.ShapeDtypeStruct(square, BF16),
-            jax.ShapeDtypeStruct(square, BF16),
+            jax.ShapeDtypeStruct((2 * RANK, RANK), BF16),
             jax.ShapeDtypeStruct(square, BF16),
         ),
         in_specs=[hbm] * 4,
-        out_specs=(vmem,) * 6,
+        out_specs=(vmem,) * 5,
         scratch_shapes=[
             pltpu.VMEM(square, BF16),
             pltpu.VMEM(wide, BF16),
@@ -428,6 +447,7 @@
             pltpu.VMEM((2, LINE, RANK), BF16),
             pltpu.VMEM((2, NX, LINE, RANK), BF16),
             pltpu.VMEM((2, LINE, RANK), F32),
+            pltpu.VMEM((2, SUB, RANK), F32),
             pltpu.VMEM((2, LINE, RANK), BF16),
             pltpu.VMEM((2, NY, SUB, RANK), BF16),
             pltpu.VMEM((2, 2, SUB, HALF), BF16),
@@ -451,16 +471,14 @@
     )(*(pltpu.with_memory_space_constraint(a, pltpu.HBM) for a in (delta, error, momentum, q)))
 
 
-def finish(left, merged, momentum, high, low, factor, new_error, new_momentum, outer_step, new_factor, e, m, s, sem):
+def finish(left, merged, momentum, mixed, factor, new_error, new_momentum, outer_step, new_factor, e, m, s, sem):
     size, count = ROWS // 8, 8
     copies = [pltpu.make_async_copy(factor, new_factor, sem.at[count, 0])]
     copies[0].start()
     for i in range(count):
         at = pl.ds(i * size, size)
         block = left[at, :]
-        approx = jnp.dot(block, high[...], preferred_element_type=F32) + jnp.dot(
-            block, low[...], preferred_element_type=F32
-        )
+        approx = jnp.dot(jnp.concatenate([block, block], axis=1), mixed[...], preferred_element_type=F32)
         e[at, :] = (merged[at, :].astype(F32) - approx).astype(BF16)
         moment = 0.9 * momentum[at, :].astype(F32) + approx
         m[at, :] = moment.astype(BF16)
@@ -472,7 +490,7 @@
         copy.wait()
 
 
-def outputs(left, merged, momentum, high, low, factor):
+def outputs(left, merged, momentum, mixed, factor):
     any_, vmem = pl.BlockSpec(memory_space=pl.ANY), pl.BlockSpec(memory_space=pltpu.VMEM)
     wide = (ROWS, RANK)
     return pl.pallas_call(
@@ -483,18 +501,18 @@
             jax.ShapeDtypeStruct(wide, BF16),
             jax.ShapeDtypeStruct((RANK, RANK), BF16),
         ),
-        in_specs=[vmem] * 6,
+        in_specs=[vmem] * 5,
         out_specs=(any_,) * 4,
         scratch_shapes=[pltpu.VMEM(wide, BF16)] * 3 + [pltpu.SemaphoreType.DMA((9, 3))],
         compiler_params=pltpu.CompilerParams(vmem_limit_bytes=24 << 20),
         cost_estimate=pl.CostEstimate(flops=4 * ROWS * RANK * RANK, bytes_accessed=6 * ROWS * RANK * 2, transcendentals=0),
         name="outputs",
-    )(left, merged, momentum, high, low, factor)
+    )(left, merged, momentum, mixed, factor)
 
 
 def body(delta, error, momentum, q_init):
-    left, merged, held, high, low, factor = gather(delta, error, momentum, q_init)
-    return outputs(left, merged, held, high, low, factor)
+    left, merged, held, mixed, factor = gather(delta, error, momentum, q_init)
+    return outputs(left, merged, held, mixed, factor)
 
 
 def solution(mesh):

time: 66.9 us -> 67.6 us (1.010)
  Pallas kernels: 66.2 us -> 66.9 us
    pallas_call x1, Pallas kernels: 62.7 us -> 63.4 us  [gather(): pl.pallas_call(exchange, out_shape=(jax.ShapeDtypeStruct(wide, BF16), jax...]
where the time goes in v4:
time: 67.6 us; the launch traced here: 67.5 us
  Pallas kernels  66.9 us (99%)
    pallas_call x1, Pallas kernels, gather(): pl.pallas_call(exchange, out_shape=(jax.ShapeDtypeStruct(wide, BF16), jax...  63.4 us
    pallas_call x1, Pallas kernels, outputs(): pl.pallas_call(finish, out_shape=(jax.ShapeDtypeStruct((1,) + wide, BF16)...  3.47 us

profile of v4, /device:TPU:1, one launch (start us, length us, event | category | flops | bytes accessed | tf_op | source)
XLA Modules:
  0.0 67.5 jit_solution(12263625527804311554)
XLA Ops:
  0.6 63.4 %gather_left.1 = (bf16[4096,256]{1,0:T(8,128)(2,1)S(1)}, bf16[4096,256]{1,0:T(8,128)(2,1)S(1)}, bf16[4096,256]{1,0:T(8,128)(2,1)S(1)}, bf16[512,256]{1,0:T(8,128)(2,1)S(1)}, bf16[256,256]{1,0:T(8,128)(2,1)S(1)}) custom-call(bf16[1,4096,256]{2,1,0:T(8,128)(2,1)} %delta.1, bf16[1,4096,256]{2,1,0:T(8,128)(2,1)} %error.1, bf16[4096,256]{1,0:T(8,128)(2,1)} %momentum.1, ...), custom_call_target="tpu_custom_call" | custom-call | flops 1610612736 | bytes 10485760 | tf_op jit(solution)/shard_map/gather_left/pallas_call | solution.py:428
  64.0 3.5 %outputs.1 = (bf16[1,4096,256]{2,1,0:T(8,128)(2,1)}, bf16[4096,256]{1,0:T(8,128)(2,1)}, bf16[4096,256]{1,0:T(8,128)(2,1)}, bf16[256,256]{1,0:T(8,128)(2,1)}) custom-call(bf16[4096,256]{1,0:T(8,128)(2,1)S(1)} %get-tuple-element.9.left, bf16[4096,256]{1,0:T(8,128)(2,1)S(1)} %get-tuple-element.10.merged, bf16[4096,256]{1,0:T(8,128)(2,1)S(1)} %get-tuple-element.11.momentum, ...), custom_call_target="tpu_custom_call" | custom-call | flops 1073741824 | bytes 12582912 | tf_op jit(solution)/shard_map/outputs/pallas_call | solution.py:496

commit v5 on v4

--- a/solution.py
+++ b/solution.py
@@ -30,73 +30,71 @@
     return pltpu.reciprocal(d, approx=True)
 
 
-def factor_block(a, between):
+def factor_block(a):
     tile = (8, 128)
     lane = lax.broadcasted_iota(jnp.int32, tile, 1)
     row = lax.broadcasted_iota(jnp.int32, tile, 0)
-    tiles = a.reshape(16, 8, 128)
-    pivots, following, rest = tiles[0], tiles[1], tiles[2:]
-    done = []
-    for g in range(16):
-        first = 8 * g
-        here = (lane >= first) & (lane < first + 8)
-
-        def column(x, c):
-            return jnp.broadcast_to(x[:, first + c:first + c + 1], tile)
-
-        def line(x, r):
-            return jnp.broadcast_to(x[r:r + 1], tile)
-
-        lefts = [column(pivots, c) for c in range(8)]
-        block = {(r, c): line(lefts[c], r) for c in range(8) for r in range(c, 8)}
-        own = jnp.where(here, jnp.where(lane - first == row, 1.0, 0.0), pivots)
-        lines = [line(own, r) for r in range(8)]
-        if g < 15:
+
+    def turn(k, tiles):
+        finished = lane >= 128 - 32 * k
+        pivots, following, rest = tiles[0], tiles[1], tiles[2:]
+        done = []
+        for g in range(4):
+            first = 8 * g
+            here = (lane >= first) & (lane < first + 8)
+
+            def column(x, c):
+                return jnp.broadcast_to(x[:, first + c:first + c + 1], tile)
+
+            def line(x, r):
+                return jnp.broadcast_to(x[r:r + 1], tile)
+
+            lefts = [column(pivots, c) for c in range(8)]
+            block = {(r, c): line(lefts[c], r) for c in range(8) for r in range(c, 8)}
+            own = jnp.where(here, jnp.where(lane - first == row, 1.0, 0.0), pivots)
+            lines = [line(own, r) for r in range(8)]
             below = [column(following, c) for c in range(8)]
             following = jnp.where(here, 0.0, following)
-        diag = jnp.ones(tile, F32)
-        upper = own
-        inverses = []
-        for p in range(0, 8, 2):
-            q = p + 1
-            d_p, d_pq, d_q = block[p, p], block[q, p], block[q, q]
-            det = d_p * d_q - d_pq * d_pq
-            inv_p = reciprocal(d_p)
-            inv_q = d_p * reciprocal(det)
-            ratio = d_pq * inv_p
-            inverses += [inv_p, inv_q]
-            lines[q] = lines[q] - ratio * lines[p]
-            diag = jnp.where(row == p, d_p, jnp.where(row == q, det * inv_p, diag))
-            upper = jnp.where(row == q, lines[q], upper)
-            later = range(q + 1, 8)
-            edge_p = {k: block[k, p] for k in later}
-            edge_q = {k: block[k, q] - ratio * edge_p[k] for k in later}
-            part_p = {k: edge_p[k] * inv_p for k in later}
-            part_q = {k: edge_q[k] * inv_q for k in later}
-            for c in later:
-                for r in range(c, 8):
-                    block[r, c] = block[r, c] - part_p[r] * edge_p[c] - part_q[r] * edge_q[c]
-            for k in later:
-                lines[k] = lines[k] - part_p[k] * lines[p] - part_q[k] * lines[q]
-                upper = jnp.where(row == k, lines[k], upper) if k == q + 1 else upper
-            if g < 15:
+            diag = jnp.ones(tile, F32)
+            upper = own
+            for p in range(0, 8, 2):
+                q = p + 1
+                d_p, d_pq, d_q = block[p, p], block[q, p], block[q, q]
+                det = d_p * d_q - d_pq * d_pq
+                inv_p = reciprocal(d_p)
+                inv_q = d_p * reciprocal(det)
+                ratio = d_pq * inv_p
+                lines[q] = lines[q] - ratio * lines[p]
+                diag = jnp.where(row == p, d_p, jnp.where(row == q, det * inv_p, diag))
+                upper = jnp.where(row == q, lines[q], upper)
+                later = range(q + 1, 8)
+                edge_p = {k: block[k, p] for k in later}
+                edge_q = {k: block[k, q] - ratio * edge_p[k] for k in later}
+                part_p = {k: edge_p[k] * inv_p for k in later}
+                part_q = {k: edge_q[k] * inv_q for k in later}
+                for c in later:
+                    for r in range(c, 8):
+                        block[r, c] = block[r, c] - part_p[r] * edge_p[c] - part_q[r] * edge_q[c]
+                for k in later:
+                    lines[k] = lines[k] - part_p[k] * lines[p] - part_q[k] * lines[q]
+                if p < 6:
+                    upper = jnp.where(row == q + 1, lines[q + 1], upper)
                 below_p = below[p] * inv_p
                 below_q = (below[q] - below_p * d_pq) * inv_q
                 following = following - below_p * lines[p] - below_q * lines[q]
                 for k in later:
                     below[k] = below[k] - below_p * edge_p[k] - below_q * edge_q[k]
-        done.append(jnp.where(lane <= row + first, upper * (1.0 / jnp.sqrt(diag)), 0.0))
-        if g < 14:
-            factors = (upper / diag).T[first + 16:].reshape(rest.shape[0], 8, 8)
+            done.append(jnp.where((lane <= row + first) | finished, upper * (1.0 / jnp.sqrt(diag)), 0.0))
+            factors = jnp.where(finished, 0.0, upper / diag).T[first + 16:].reshape(rest.shape[0], 8, 8)
             rest = jnp.where(here, 0.0, rest)
             for c in range(8):
                 rest = rest - factors[:, :, c:c + 1] * lines[c]
-            pivots, following, rest = following, rest[0], rest[1:] if g < 13 else None
-        elif g == 14:
-            pivots = following
-        if g in between:
-            between[g]()
-    return jnp.concatenate(done, axis=0)
+            if g < 3:
+                pivots, following, rest = following, rest[0], rest[1:]
+        tiles = [following] + [rest[t] for t in range(11)] + done
+        return jnp.stack([pltpu.roll(x, 96, 1) for x in tiles])
+
+    return lax.fori_loop(0, 4, turn, a.reshape(16, 8, 128)).reshape(128, 128)
 
 
 def inverse_factor(gram, between):
@@ -104,10 +102,11 @@
     diagonal = jnp.where(on, gram, 0.0)
     scale = 1.0 / jnp.sqrt(jnp.sum(diagonal, axis=0, keepdims=True))
     gram = gram * scale * (1.0 / jnp.sqrt(jnp.sum(diagonal, axis=1, keepdims=True)))
-    w11 = factor_block(gram[:128, :128], between[0])
+    w11 = factor_block(gram[:128, :128])
+    between()
     l21 = mm(gram[128:, :128], w11, ((1,), (1,)))
     corner = mm(l21, w11, ((1,), (0,)))
-    w22 = factor_block(gram[128:, 128:] - mm(l21, l21, ((1,), (1,))), between[1])
+    w22 = factor_block(gram[128:, 128:] - mm(l21, l21, ((1,), (1,))))
     w21 = -mm(w22, corner, ((1,), (0,)))
     top = jnp.concatenate([w11, jnp.zeros((128, 128), F32)], axis=1)
     return jnp.concatenate([top, jnp.concatenate([w21, w22], axis=1)], axis=0) * scale
@@ -152,7 +151,7 @@
     def line(h, i):
         return h * PART + turn(c1[h], i, NX) * LINE
 
-    order = [(whose, i) for whose in range(2) for i in (2, 1, 3, 0)]
+    order = [(whose, i) for whose in range(2) for i in (2, 3, 1, 0)]
 
     def loads(whose, i, h):
         src, k = rows((mine if whose else theirs) + line(h, i), LINE), whose * NX + i
@@ -221,22 +220,24 @@
             both = total.astype(BF16)
             xs[turn(y, i, NY)] = both.reshape(NX, SUB, RANK)
             total = jnp.dot(both, q[...], preferred_element_type=F32)
-        if i:
+        if not isinstance(i, int):
             s1[here, :] = total.astype(BF16)
             go("first", s1.at[here], r1.at[h, c1[h]], p1r.at[h], peer1(h, turn(c1[h], i, NX)))
         else:
             o1[h] = total
 
-    for n, (whose, i) in enumerate(order):
-        if n == 0:
-            pl.semaphore_wait(barrier, len(greeted))
-        if n == 2:
+    pl.semaphore_wait(barrier, len(greeted))
+    for step in (give, take):
+        if step is take:
             load_q.wait()
+
+        @pl.loop(0, NX - 1)
+        def _(n, step=step):
+            for h in range(2):
+                step(1 + lax.rem(n + 1, NX - 1), h)
+
         for h in range(2):
-            if whose:
-                take(i, h)
-            else:
-                give(i, h)
+            step(0, h)
 
     load_momentum = pltpu.make_async_copy(momentum, held, ld.at[9])
     load_momentum.start()
@@ -396,7 +397,7 @@
     sent("gather", span(left, 6 * SUB))
     sent("lines", span(left, 24 * SUB))
     landed(gin, oner.at[4])
-    inverse = inverse_factor(gsum[...] + gin[...], ({}, {3: add_across}))
+    inverse = inverse_factor(gsum[...] + gin[...], add_across)
     landed(span(zall, (OWNERS - 1) * PIECE), oner.at[7])
     w1 = inverse.astype(BF16)
     w2 = (inverse - w1.astype(F32)).astype(BF16)

time: 67.6 us -> 68.2 us (level)
  no operation moved by 1% of the time
where the time goes in v5:
time: 68.2 us; the launch traced here: 68.1 us
  Pallas kernels  67.5 us (99%)
    pallas_call x1, Pallas kernels, gather(): pl.pallas_call(exchange, out_shape=(jax.ShapeDtypeStruct(wide, BF16), jax...  64 us
    pallas_call x1, Pallas kernels, outputs(): pl.pallas_call(finish, out_shape=(jax.ShapeDtypeStruct((1,) + wide, BF16)...  3.47 us

profile of v5, /device:TPU:1, one launch (start us, length us, event | category | flops | bytes accessed | tf_op | source)
XLA Modules:
  0.0 68.1 jit_solution(12345204575844508385)
XLA Ops:
  0.6 64.0 %gather_left.1 = (bf16[4096,256]{1,0:T(8,128)(2,1)S(1)}, bf16[4096,256]{1,0:T(8,128)(2,1)S(1)}, bf16[4096,256]{1,0:T(8,128)(2,1)S(1)}, bf16[512,256]{1,0:T(8,128)(2,1)S(1)}, bf16[256,256]{1,0:T(8,128)(2,1)S(1)}) custom-call(bf16[1,4096,256]{2,1,0:T(8,128)(2,1)} %delta.1, bf16[1,4096,256]{2,1,0:T(8,128)(2,1)} %error.1, bf16[4096,256]{1,0:T(8,128)(2,1)} %momentum.1, ...), custom_call_target="tpu_custom_call" | custom-call | flops 1610612736 | bytes 10485760 | tf_op jit(solution)/shard_map/gather_left/pallas_call | solution.py:429
  64.7 3.5 %outputs.1 = (bf16[1,4096,256]{2,1,0:T(8,128)(2,1)}, bf16[4096,256]{1,0:T(8,128)(2,1)}, bf16[4096,256]{1,0:T(8,128)(2,1)}, bf16[256,256]{1,0:T(8,128)(2,1)}) custom-call(bf16[4096,256]{1,0:T(8,128)(2,1)S(1)} %get-tuple-element.9.left, bf16[4096,256]{1,0:T(8,128)(2,1)S(1)} %get-tuple-element.10.merged, bf16[4096,256]{1,0:T(8,128)(2,1)S(1)} %get-tuple-element.11.momentum, ...), custom_call_target="tpu_custom_call" | custom-call | flops 1073741824 | bytes 12582912 | tf_op jit(solution)/shard_map/outputs/pallas_call | solution.py:497

commit v6 on v5

--- a/solution.py
+++ b/solution.py
@@ -151,7 +151,7 @@
     def line(h, i):
         return h * PART + turn(c1[h], i, NX) * LINE
 
-    order = [(whose, i) for whose in range(2) for i in (2, 3, 1, 0)]
+    order = [(whose, i) for whose in range(2) for i in (2, 1, 3, 0)]
 
     def loads(whose, i, h):
         src, k = rows((mine if whose else theirs) + line(h, i), LINE), whose * NX + i
@@ -220,24 +220,22 @@
             both = total.astype(BF16)
             xs[turn(y, i, NY)] = both.reshape(NX, SUB, RANK)
             total = jnp.dot(both, q[...], preferred_element_type=F32)
-        if not isinstance(i, int):
+        if i:
             s1[here, :] = total.astype(BF16)
             go("first", s1.at[here], r1.at[h, c1[h]], p1r.at[h], peer1(h, turn(c1[h], i, NX)))
         else:
             o1[h] = total
 
-    pl.semaphore_wait(barrier, len(greeted))
-    for step in (give, take):
-        if step is take:
+    for n, (whose, i) in enumerate(order):
+        if n == 0:
+            pl.semaphore_wait(barrier, len(greeted))
+        if n == 2:
             load_q.wait()
-
-        @pl.loop(0, NX - 1)
-        def _(n, step=step):
-            for h in range(2):
-                step(1 + lax.rem(n + 1, NX - 1), h)
-
         for h in range(2):
-            step(0, h)
+            if whose:
+                take(i, h)
+            else:
+                give(i, h)
 
     load_momentum = pltpu.make_async_copy(momentum, held, ld.at[9])
     load_momentum.start()
@@ -259,6 +257,9 @@
                 go("second", s2.at[h, at], r2.at[h, c2[h]], p2r.at[h], peer2(h, b))
             else:
                 o2[h] = total
+    for i in (2, 1, 3):
+        b = turn(x, i, NX)
+        go("merged", xs.at[:, b], rx.at[x], oner.at[1], device(b, y, z, core))
     for h in range(2):
         landed(r2.at[h, pl.ds(0, NY - 1)], p2r.at[h])
         total = o2[h]
@@ -277,9 +278,6 @@
         b = turn(z, i, NZ)
         c, at = spot(b)
         go("z", s3.at[:, c, at], r3.at[z], oner.at[0], device(x, y, b, core))
-    for i in (2, 1, 3):
-        b = turn(x, i, NX)
-        go("merged", xs.at[:, b], rx.at[x], oner.at[1], device(b, y, z, core))
     sent("core", span(left, 2 * PART))
     sent("first", span(left, 6 * LINE))
     sent("second", span(left, 6 * SUB))
@@ -327,26 +325,26 @@
             b = turn(c2[h], i, NY)
             go("gather", at, at, a2r.at[h, c2[h]], peer2(h, b))
         along(h, 0)
+    for j in (1, 3, 2):
+        for h in range(2):
+            at, b = left.at[sub(h, 0, j)], turn(c2[h], j, NY)
+            landed(at, a2r.at[h, b])
+            along(h, j)
+    for h in range(2):
+        cross(h, 0)
+
+    owner = x * 2 + core
+    others = [(turn(x, i, NX), lax.rem(core + e, 2)) for i in range(NX) for e in range(2) if i or e]
+
+    def piece(v, c):
+        return rows((v * 2 + c) * PIECE, PIECE)
+
+    total = across_rows(left[rows(mine + line(0, 0), LINE), :], sx[0])
     landed(span(rx, NX - 1), oner.at[1])
     owned = xs[:, x].astype(F32)
     for i in range(1, NX):
         owned += rx[turn(x, i, NX)].astype(F32)
     sx[1] = owned.astype(BF16).reshape(LINE, RANK)
-    for j in (1, 3, 2):
-        for h in range(2):
-            at, b = left.at[sub(h, 0, j)], turn(c2[h], j, NY)
-            landed(at, a2r.at[h, b])
-            along(h, j)
-    for h in range(2):
-        cross(h, 0)
-
-    owner = x * 2 + core
-    others = [(turn(x, i, NX), lax.rem(core + e, 2)) for i in range(NX) for e in range(2) if i or e]
-
-    def piece(v, c):
-        return rows((v * 2 + c) * PIECE, PIECE)
-
-    total = across_rows(left[rows(mine + line(0, 0), LINE), :], sx[0])
     for i in (1, 3, 2):
         arrive(1, i, 0)
     owned = jnp.concatenate([left[rows(mine + PART + v * LINE + x * SUB, SUB), :] for v in range(NY)], axis=0)

time: 68.2 us -> 69.5 us (1.019)
  Pallas kernels: 67.5 us -> 68.8 us
    pallas_call x1, Pallas kernels: 64 us -> 65.3 us  [gather(): pl.pallas_call(exchange, out_shape=(jax.ShapeDtypeStruct(wide, BF16), jax...]
where the time goes in v6:
time: 69.5 us
  Pallas kernels  68.8 us (99%)
    pallas_call x1, Pallas kernels, gather(): pl.pallas_call(exchange, out_shape=(jax.ShapeDtypeStruct(wide, BF16), jax...  65.3 us
    pallas_call x1, Pallas kernels, outputs(): pl.pallas_call(finish, out_shape=(jax.ShapeDtypeStruct((1,) + wide, BF16)...  3.47 us

profile of v6, /device:TPU:1, one launch (start us, length us, event | category | flops | bytes accessed | tf_op | source)
XLA Modules:
  0.0 69.5 jit_solution(17570212941090353794)
XLA Ops:
  0.6 65.3 %gather_left.1 = (bf16[4096,256]{1,0:T(8,128)(2,1)S(1)}, bf16[4096,256]{1,0:T(8,128)(2,1)S(1)}, bf16[4096,256]{1,0:T(8,128)(2,1)S(1)}, bf16[512,256]{1,0:T(8,128)(2,1)S(1)}, bf16[256,256]{1,0:T(8,128)(2,1)S(1)}) custom-call(bf16[1,4096,256]{2,1,0:T(8,128)(2,1)} %delta.1, bf16[1,4096,256]{2,1,0:T(8,128)(2,1)} %error.1, bf16[4096,256]{1,0:T(8,128)(2,1)} %momentum.1, ...), custom_call_target="tpu_custom_call" | custom-call | flops 1610612736 | bytes 10485760 | tf_op jit(solution)/shard_map/gather_left/pallas_call | solution.py:427
  66.0 3.5 %outputs.1 = (bf16[1,4096,256]{2,1,0:T(8,128)(2,1)}, bf16[4096,256]{1,0:T(8,128)(2,1)}, bf16[4096,256]{1,0:T(8,128)(2,1)}, bf16[256,256]{1,0:T(8,128)(2,1)}) custom-call(bf16[4096,256]{1,0:T(8,128)(2,1)S(1)} %get-tuple-element.9.left, bf16[4096,256]{1,0:T(8,128)(2,1)S(1)} %get-tuple-element.10.merged, bf16[4096,256]{1,0:T(8,128)(2,1)S(1)} %get-tuple-element.11.momentum, ...), custom_call_target="tpu_custom_call" | custom-call | flops 1073741824 | bytes 12582912 | tf_op jit(solution)/shard_map/outputs/pallas_call | solution.py:495

commit v7 on v3

--- a/solution.py
+++ b/solution.py
@@ -376,7 +376,7 @@
     sent("gather", span(left, 6 * SUB))
     sent("lines", span(left, 24 * SUB))
     landed(gin, oner.at[4])
-    inverse = inverse_factor(gsum[...] + gin[...], ({}, {3: add_across}))
+    inverse = inverse_factor(gsum[...] + gin[...], ({}, {0: add_across}))
     landed(span(zall, (OWNERS - 1) * PIECE), oner.at[7])
     w1 = inverse.astype(BF16)
     w2 = (inverse - w1.astype(F32)).astype(BF16)

time: 66.9 us -> 66.8 us (level)
  no operation moved by 1% of the time
where the time goes in v7:
time: 66.8 us; the launch traced here: 66.7 us
  Pallas kernels  66.1 us (99%)
    pallas_call x1, Pallas kernels, gather(): pl.pallas_call(exchange, out_shape=(jax.ShapeDtypeStruct(wide, BF16), jax...  62.6 us
    pallas_call x1, Pallas kernels, outputs(): pl.pallas_call(finish, out_shape=(jax.ShapeDtypeStruct((1,) + wide, BF16)...  3.47 us

profile of v7, /device:TPU:1, one launch (start us, length us, event | category | flops | bytes accessed | tf_op | source)
XLA Modules:
  0.0 66.7 jit_solution(1433197417735326618)
XLA Ops:
  0.6 62.6 %gather_left.1 = (bf16[4096,256]{1,0:T(8,128)(2,1)S(1)}, bf16[4096,256]{1,0:T(8,128)(2,1)S(1)}, bf16[4096,256]{1,0:T(8,128)(2,1)S(1)}, bf16[256,256]{1,0:T(8,128...) custom-call(bf16[1,4096,256]{2,1,0:T(8,128)(2,1)} %delta.1, bf16[1,4096,256]{2,1,0:T(8,128)(2,1)} %error.1, ...), custom_call_target="tpu_custom_call" | custom-call | flops 1610612736 | bytes 10485760 | tf_op jit(solution)/shard_map/gather_left/pallas_call | solution.py:408
  63.3 3.5 %outputs.1 = (bf16[1,4096,256]{2,1,0:T(8,128)(2,1)}, bf16[4096,256]{1,0:T(8,128)(2,1)}, bf16[4096,256]{1,0:T(8,128)(2,1)}, bf16[256,256]{1,0:T(8,128)(2,1)}) custom-call(bf16[4096,256]{1,0:T(8,128)(2,1)S(1)} %get-tuple-element.10.left, bf16[4096,256]{1,0:T(8,128)(2,1)S(1)} %get-tuple-element.11.merged, bf16[4096,256]{1,0:T(8,128)(2,1)S(1)} %get-tuple-element.12.momentum, ...), custom_call_target="tpu_custom_call" | custom-call | flops 1073741824 | bytes 12582912 | tf_op jit(solution)/shard_map/outputs/pallas_call | solution.py:478
